TPU v7x, 768 devices: a whole 4x8x12 slice. The times are simulated.
768 devices in a mesh: row: 128 (over x, y, z_hi, core), col: 6 (over z_lo).
Axes of the slice: x: 4, y: 8, z: 12 (z_hi: 2, z_lo: 6; z = z_hi * 6 + z_lo), core: 2. Of those that a mesh axis runs over, the one named last changes fastest.
Arguments:
- vectors: float32 [8, 9437184], P(None, ('row', 'col')), may hold values from -6 to 6
- tiles: bfloat16 [49152, 128, 128], P(('row', 'col')), may hold values from -0.25 to 0.25
- tile_rows: int32 [49152], P(('row', 'col')), may hold values from 0 to 73727, as said below
- tile_cols: int32 [49152], P(('row', 'col')), may hold values from 0 to 73727, as said below
- row_counts: int32 [49152], P(('row', 'col')), may hold values from 1 to 128, as said below
- live_tiles: int32 [768], P(('row', 'col')), may hold values from 1 to 64, as said below
Outputs:
- product: float32 [8, 9437184], P(None, ('row', 'col'))
Inputs may be any that keep to these rules, and one draw needn't show every extreme that they name: `tile_rows`: A slot of device d (row index rr, col index cc) has a tile row in its row band, rr * 6 * 96 up to (rr + 1) * 6 * 96 - 1; a slot beyond the device's live count repeats the coordinates of the device's first slot. `tile_cols`: A slot's tile column j satisfies (j // 96) % 6 == cc, j // 576 lies between rr and rr + 6, and j >= its tile row; places may repeat. `row_counts`: slot 0 of every device has 128 rows. `live_tiles`: live slots are the first of each device; device 0 has all 64 live.
All inputs are finite; a program needn't handle non-finite values.
Results may differ from a plain program's by a relative error of at most 0.0029.
Values may be sent and summed in bfloat16 or wider, within the bound.
No kernel may reach another device: no remote copies, remote signals or barrier semaphores. Data moves between devices by JAX's collectives and lax.ppermute only.
A program may use at most 32 MiB of HBM per device.

v0:
```python
import jax
import jax.numpy as jnp
from jax import lax
from jax.sharding import PartitionSpec as P

REACH = 6


def from_behind(value, axis, by):
    devices = lax.axis_size(axis)
    pairs = [(i, i + by) for i in range(devices) if 0 <= i + by < devices]
    return lax.ppermute(value, axis, pairs)


def local(vectors, tiles, tile_rows, tile_cols, row_counts, live_tiles):
    vec_count = vectors.shape[0]
    seg_len = vectors.shape[1]
    slot_count = tiles.shape[0]
    tile_len = tiles.shape[1]
    col_devices = lax.axis_size("col")
    per_piece = seg_len // tile_len
    band_rows = col_devices * per_piece
    window = (REACH + 1) * per_piece
    group_len = min(32, slot_count)
    row_place = lax.axis_index("row")
    local_rows = jnp.clip(tile_rows - row_place * band_rows, 0, band_rows - 1)
    local_cols = jnp.clip(
        (tile_cols // band_rows - row_place) * per_piece + tile_cols % per_piece, 0, window - 1
    )
    live_count = live_tiles[0]
    slot_ids = jnp.arange(slot_count, dtype=jnp.int32)
    counts = jnp.where(slot_ids < live_count, row_counts, 0)
    lane_ids = jnp.arange(tile_len, dtype=jnp.int32)
    rounded = vectors.astype(jnp.bfloat16)
    row_band = lax.all_gather(rounded, "col", axis=1, tiled=True).reshape(
        vec_count, band_rows, tile_len
    )
    pieces = [rounded]
    for offset in range(1, REACH + 1):
        pieces.append(from_behind(rounded, "row", -offset))
    columns = jnp.concatenate(pieces, axis=1).reshape(vec_count, window, tile_len)

    def apply_group(number, totals):
        row_acc, col_acc = totals
        first_slot = number * group_len
        block_tiles = lax.dynamic_slice_in_dim(tiles, first_slot, group_len, 0)
        rows_here = lax.dynamic_slice_in_dim(local_rows, first_slot, group_len, 0)
        cols_here = lax.dynamic_slice_in_dim(local_cols, first_slot, group_len, 0)
        counts_here = lax.dynamic_slice_in_dim(counts, first_slot, group_len, 0)
        row_mask = lane_ids[None, :] < counts_here[:, None]
        inputs = jnp.take(columns, cols_here, axis=1)
        forward = jnp.einsum(
            "tik,btk->bti", block_tiles, inputs, preferred_element_type=jnp.float32
        )
        forward = jnp.where(row_mask[None], forward, jnp.zeros((), jnp.float32))
        row_acc = row_acc.at[:, rows_here].add(forward)
        partner = jnp.where(
            row_mask[None], jnp.take(row_band, rows_here, axis=1), jnp.zeros((), jnp.bfloat16)
        )
        mirror = jnp.einsum(
            "tik,bti->btk", block_tiles, partner, preferred_element_type=jnp.float32
        )
        col_acc = col_acc.at[:, cols_here].add(mirror)
        return (row_acc, col_acc)

    group_count = (live_count + group_len - 1) // group_len
    start_totals = (
        jnp.zeros((vec_count, band_rows, tile_len), jnp.float32),
        jnp.zeros((vec_count, window, tile_len), jnp.float32),
    )
    row_acc, col_acc = lax.fori_loop(0, group_count, apply_group, start_totals)
    mirror_parts = col_acc.reshape(vec_count, REACH + 1, per_piece * tile_len)
    window_sum = mirror_parts[:, 0]
    for offset in range(1, REACH + 1):
        window_sum = window_sum + from_behind(mirror_parts[:, offset], "row", offset)
    row_part = lax.psum_scatter(
        row_acc.reshape(vec_count, band_rows * tile_len), "col", scatter_dimension=1, tiled=True
    )
    return row_part + window_sum


def solution(mesh):
    placed = (
        P(None, ("row", "col")),
        P(("row", "col"), None, None),
        P(("row", "col")),
        P(("row", "col")),
        P(("row", "col")),
        P(("row", "col")),
    )
    return jax.shard_map(
        local, mesh=mesh, in_specs=placed, out_specs=P(None, ("row", "col")), check_vma=False
    )
```

profile of v0, /device:TPU:155, one launch (start us, length us, event | category | flops | bytes accessed | tf_op | source)
XLA Modules:
  0.0 284.1 jit_solution(15270884019050813122)
XLA Ops:
  8.3 12.2 %collective-permute-start.5 = (bf16[8,12288]{1,0:T(8,128)(2,1)}, bf16[8,12288]{1,0:T(8,128)(2,1)S(1)}, u32[]{:S(2)}, u32[]{:S(2)}) collective-permute-start(bf16[8,12288]{1,0:T(8,128)(2,1)} %get-tuple-element.114), channel_id=1, source_target_pairs={{36,0},{42,6},{48,12},{54,18},{60,24},{66,30},{72,36},{78,42},{84,... | collective-permute-start | bytes 589832 | tf_op jit(solution)/shard_map/ppermute | solution.py:12
  20.5 2.9 %collective-permute-start.4 = (bf16[8,12288]{1,0:T(8,128)(2,1)}, bf16[8,12288]{1,0:T(8,128)(2,1)S(1)}, u32[]{:S(2)}, u32[]{:S(2)}) collective-permute-start(bf16[8,12288]{1,0:T(8,128)(2,1)} %get-tuple-element.114), channel_id=1, source_target_pairs={{30,0},{36,6},{42,12},{48,18},{54,24},{60,30},{66,36},{72,42},{78,... | collective-permute-start | bytes 589832 | tf_op jit(solution)/shard_map/ppermute | solution.py:12
  23.5 5.1 %collective-permute-start.3 = (bf16[8,12288]{1,0:T(8,128)(2,1)}, bf16[8,12288]{1,0:T(8,128)(2,1)S(1)}, u32[]{:S(2)}, u32[]{:S(2)}) collective-permute-start(bf16[8,12288]{1,0:T(8,128)(2,1)} %get-tuple-element.114), channel_id=1, source_target_pairs={{24,0},{30,6},{36,12},{42,18},{48,24},{54,30},{60,36},{66,42},{72,... | collective-permute-start | bytes 589832 | tf_op jit(solution)/shard_map/ppermute | solution.py:12
  28.5 9.9 %collective-permute-start.2 = (bf16[8,12288]{1,0:T(8,128)(2,1)}, bf16[8,12288]{1,0:T(8,128)(2,1)S(1)}, u32[]{:S(2)}, u32[]{:S(2)}) collective-permute-start(bf16[8,12288]{1,0:T(8,128)(2,1)} %get-tuple-element.114), channel_id=1, source_target_pairs={{18,0},{24,6},{30,12},{36,18},{42,24},{48,30},{54,36},{60,42},{66,... | collective-permute-start | bytes 589832 | tf_op jit(solution)/shard_map/ppermute | solution.py:12
  38.5 1.9 collective-permute-start
  42.4 22.9 %collective-permute-done = bf16[8,12288]{1,0:T(8,128)(2,1)S(1)} collective-permute-done((bf16[8,12288]{1,0:T(8,128)(2,1)}, bf16[8,12288]{1,0:T(8,128)(2,1)S(1)}, u32[]{:S(2)}, u32[]{:S(2)}) %collective-permute-start) | collective-permute-done | bytes 196640 | tf_op jit(solution)/shard_map/ppermute | solution.py:12
  65.3 21.2 %collective-permute-start.1 = (bf16[8,12288]{1,0:T(8,128)(2,1)}, bf16[8,12288]{1,0:T(8,128)(2,1)S(1)}, u32[]{:S(2)}, u32[]{:S(2)}) collective-permute-start(bf16[8,12288]{1,0:T(8,128)(2,1)} %get-tuple-element.114), channel_id=1, source_target_pairs={{12,0},{18,6},{24,12},{30,18},{36,24},{42,30},{48,36},{54,42},{60,... | collective-permute-start | bytes 589832 | tf_op jit(solution)/shard_map/ppermute | solution.py:12
  86.6 5.0 %collective-permute-done.1 = bf16[8,12288]{1,0:T(8,128)(2,1)S(1)} collective-permute-done((bf16[8,12288]{1,0:T(8,128)(2,1)}, bf16[8,12288]{1,0:T(8,128)(2,1)S(1)}, u32[]{:S(2)}, u32[]{:S(2)}) %collective-permute-start.1) | collective-permute-done | bytes 196640 | tf_op jit(solution)/shard_map/ppermute | solution.py:12
  94.4 1.7 broadcast_in_dim.61
  97.0 13.2 %while.13 = (s32[]{:T(128)}, f32[8,576,128]{2,0,1:T(8,128)}, f32[8,672,128]{2,0,1:T(8,128)}, s32[]{:T(128)}, s32[64]{0:T(128)S(1)}, /*index=5*/s32[64]{0:T(128)S...) while((s32[]{:T(128)}, f32[8,576,128]{2,0,1:T(8,128)}, ...), condition=%wide.region_3.4_spmd.clone, body=%wide.region_0.3_spmd.clone.sunk | while | flops 16980356 | bytes 3562371 | solution.py:71
  97.3 1.9 gather_fusion
  99.2 1.9 gather_fusion.1
  102.2 4.0 %scatter_fusion = f32[8,576,128]{2,0,1:T(8,128)} fusion(f32[8,576,128]{2,0,1:T(8,128)} %get-tuple-element.210, s32[32]{0:T(128)S(1)} %get-tuple-element.191, f32[32,8,128]{2,1,0:T(8,128)S(1)} %convolution_select_fusion.2), kind=kCustom, calls=%fused_computation.2.clone.clone.1 | custom fusion | flops 32768 | bytes 393344 | tf_op jit(solution)/shard_map/while/body/scatter-add | solution.py:56
  106.2 4.0 %scatter_fusion.1 = f32[8,672,128]{2,0,1:T(8,128)} fusion(f32[8,672,128]{2,0,1:T(8,128)} %get-tuple-element.211, s32[32]{0:T(128)S(1)} %get-tuple-element.192, f32[32,8,128]{2,1,0:T(8,128)S(1)} %fusion.39), kind=kCustom, calls=%fused_computation.3.clone.clone.1 | custom fusion | flops 32768 | bytes 393344 | tf_op jit(solution)/shard_map/while/body/scatter-add | solution.py:63
  110.3 1.7 slice_bitcast_fusion.5
  112.0 2.9 %collective-permute-start.6 = (f32[8,12288]{1,0:T(8,128)S(1)}, f32[8,12288]{1,0:T(8,128)S(1)}, u32[]{:S(2)}, u32[]{:S(2)}) collective-permute-start(f32[8,12288]{1,0:T(8,128)S(1)} %get-tuple-element.117), channel_id=1, source_target_pairs={{0,6},{6,12},{12,18},{18,24},{24,30},{30,36},{36,42},{42,48},{48,5... | collective-permute-start | bytes 1179656 | tf_op jit(solution)/shard_map/ppermute | solution.py:12
  115.0 21.0 %collective-permute-start.11 = (f32[8,12288]{1,0:T(8,128)S(1)}, f32[8,12288]{1,0:T(8,128)S(1)}, u32[]{:S(2)}, u32[]{:S(2)}) collective-permute-start(f32[8,12288]{1,0:T(8,128)S(1)} %get-tuple-element.118), channel_id=1, source_target_pairs={{0,36},{6,42},{12,48},{18,54},{24,60},{30,66},{36,72},{42,78},{48,... | collective-permute-start | bytes 1179656 | tf_op jit(solution)/shard_map/ppermute | solution.py:12
  136.0 3.4 %collective-permute-start.10 = (f32[8,12288]{1,0:T(8,128)S(1)}, f32[8,12288]{1,0:T(8,128)S(1)}, u32[]{:S(2)}, u32[]{:S(2)}) collective-permute-start(f32[8,12288]{1,0:T(8,128)S(1)} %get-tuple-element.119), channel_id=1, source_target_pairs={{0,30},{6,36},{12,42},{18,48},{24,54},{30,60},{36,66},{42,72},{48,... | collective-permute-start | bytes 1179656 | tf_op jit(solution)/shard_map/ppermute | solution.py:12
  139.5 4.5 %collective-permute-start.9 = (f32[8,12288]{1,0:T(8,128)S(1)}, f32[8,12288]{1,0:T(8,128)S(1)}, u32[]{:S(2)}, u32[]{:S(2)}) collective-permute-start(f32[8,12288]{1,0:T(8,128)S(1)} %get-tuple-element.120), channel_id=1, source_target_pairs={{0,24},{6,30},{12,36},{18,42},{24,48},{30,54},{36,60},{42,66},{48,... | collective-permute-start | bytes 1179656 | tf_op jit(solution)/shard_map/ppermute | solution.py:12
  144.0 2.6 collective-permute-start.8
  146.7 45.2 %collective-permute-start.7 = (f32[8,12288]{1,0:T(8,128)S(1)}, f32[8,12288]{1,0:T(8,128)S(1)}, u32[]{:S(2)}, u32[]{:S(2)}) collective-permute-start(f32[8,12288]{1,0:T(8,128)S(1)} %get-tuple-element.122), channel_id=1, source_target_pairs={{0,12},{6,18},{12,24},{18,30},{24,36},{30,42},{36,48},{42,54},{48,... | collective-permute-start | bytes 1179656 | tf_op jit(solution)/shard_map/ppermute | solution.py:12
  191.8 47.7 %collective-permute-done.11 = f32[8,12288]{1,0:T(8,128)S(1)} collective-permute-done((f32[8,12288]{1,0:T(8,128)S(1)}, f32[8,12288]{1,0:T(8,128)S(1)}, u32[]{:S(2)}, u32[]{:S(2)}) %collective-permute-start.11) | collective-permute-done | bytes 393248 | tf_op jit(solution)/shard_map/ppermute | solution.py:12
  239.6 35.7 %collective-permute-done.7 = f32[8,12288]{1,0:T(8,128)S(1)} collective-permute-done((f32[8,12288]{1,0:T(8,128)S(1)}, f32[8,12288]{1,0:T(8,128)S(1)}, u32[]{:S(2)}, u32[]{:S(2)}) %collective-permute-start.7) | collective-permute-done | bytes 393248 | tf_op jit(solution)/shard_map/ppermute | solution.py:12
  275.3 2.0 fusion.27
  (35 shorter events, 8.1 us)
Async XLA Ops:
  6.5 85.2 %all-gather.2.cloned.1.call-start = ((), (), s32[]{:S(2)}) async-start(), calls=%async_computation.1 | async-start | bytes 1376256 | tf_op jit(solution)/shard_map/all_gather | solution.py:35
  8.3 267.0 %reduce-scatter.2.cloned.1.call-start = ((), (), s32[]{:S(2)}) async-start(), calls=%async_computation.2 | async-start | bytes 2752512 | tf_op jit(solution)/shard_map/reduce_scatter | solution.py:76
  8.3 83.4 %collective-permute-start.5 = (bf16[8,12288]{1,0:T(8,128)(2,1)}, bf16[8,12288]{1,0:T(8,128)(2,1)S(1)}, u32[]{:S(2)}, u32[]{:S(2)}) collective-permute-start(bf16[8,12288]{1,0:T(8,128)(2,1)} %get-tuple-element.114), channel_id=1, source_target_pairs={{36,0},{42,6},{48,12},{54,18},{60,24},{66,30},{72,36},{78,42},{84,... | collective-permute-start | bytes 589832 | tf_op jit(solution)/shard_map/ppermute | solution.py:12
  20.5 71.1 %collective-permute-start.4 = (bf16[8,12288]{1,0:T(8,128)(2,1)}, bf16[8,12288]{1,0:T(8,128)(2,1)S(1)}, u32[]{:S(2)}, u32[]{:S(2)}) collective-permute-start(bf16[8,12288]{1,0:T(8,128)(2,1)} %get-tuple-element.114), channel_id=1, source_target_pairs={{30,0},{36,6},{42,12},{48,18},{54,24},{60,30},{66,36},{72,42},{78,... | collective-permute-start | bytes 589832 | tf_op jit(solution)/shard_map/ppermute | solution.py:12
  23.5 68.2 %collective-permute-start.3 = (bf16[8,12288]{1,0:T(8,128)(2,1)}, bf16[8,12288]{1,0:T(8,128)(2,1)S(1)}, u32[]{:S(2)}, u32[]{:S(2)}) collective-permute-start(bf16[8,12288]{1,0:T(8,128)(2,1)} %get-tuple-element.114), channel_id=1, source_target_pairs={{24,0},{30,6},{36,12},{42,18},{48,24},{54,30},{60,36},{66,42},{72,... | collective-permute-start | bytes 589832 | tf_op jit(solution)/shard_map/ppermute | solution.py:12
  28.5 63.1 %collective-permute-start.2 = (bf16[8,12288]{1,0:T(8,128)(2,1)}, bf16[8,12288]{1,0:T(8,128)(2,1)S(1)}, u32[]{:S(2)}, u32[]{:S(2)}) collective-permute-start(bf16[8,12288]{1,0:T(8,128)(2,1)} %get-tuple-element.114), channel_id=1, source_target_pairs={{18,0},{24,6},{30,12},{36,18},{42,24},{48,30},{54,36},{60,42},{66,... | collective-permute-start | bytes 589832 | tf_op jit(solution)/shard_map/ppermute | solution.py:12
  38.5 26.9 %collective-permute-start = (bf16[8,12288]{1,0:T(8,128)(2,1)}, bf16[8,12288]{1,0:T(8,128)(2,1)S(1)}, u32[]{:S(2)}, u32[]{:S(2)}) collective-permute-start(bf16[8,12288]{1,0:T(8,128)(2,1)} %get-tuple-element.114), channel_id=1, source_target_pairs={{6,0},{12,6},{18,12},{24,18},{30,24},{36,30},{42,36},{48,42},{54,4... | collective-permute-start | bytes 589832 | tf_op jit(solution)/shard_map/ppermute | solution.py:12
  65.3 26.2 %collective-permute-start.1 = (bf16[8,12288]{1,0:T(8,128)(2,1)}, bf16[8,12288]{1,0:T(8,128)(2,1)S(1)}, u32[]{:S(2)}, u32[]{:S(2)}) collective-permute-start(bf16[8,12288]{1,0:T(8,128)(2,1)} %get-tuple-element.114), channel_id=1, source_target_pairs={{12,0},{18,6},{24,12},{30,18},{36,24},{42,30},{48,36},{54,42},{60,... | collective-permute-start | bytes 589832 | tf_op jit(solution)/shard_map/ppermute | solution.py:12
  91.7 1.1 copy-start.1
  94.4 2.6 copy-start
  112.0 34.6 %collective-permute-start.6 = (f32[8,12288]{1,0:T(8,128)S(1)}, f32[8,12288]{1,0:T(8,128)S(1)}, u32[]{:S(2)}, u32[]{:S(2)}) collective-permute-start(f32[8,12288]{1,0:T(8,128)S(1)} %get-tuple-element.117), channel_id=1, source_target_pairs={{0,6},{6,12},{12,18},{18,24},{24,30},{30,36},{36,42},{42,48},{48,5... | collective-permute-start | bytes 1179656 | tf_op jit(solution)/shard_map/ppermute | solution.py:12
  115.0 124.6 %collective-permute-start.11 = (f32[8,12288]{1,0:T(8,128)S(1)}, f32[8,12288]{1,0:T(8,128)S(1)}, u32[]{:S(2)}, u32[]{:S(2)}) collective-permute-start(f32[8,12288]{1,0:T(8,128)S(1)} %get-tuple-element.118), channel_id=1, source_target_pairs={{0,36},{6,42},{12,48},{18,54},{24,60},{30,66},{36,72},{42,78},{48,... | collective-permute-start | bytes 1179656 | tf_op jit(solution)/shard_map/ppermute | solution.py:12
  136.0 103.6 %collective-permute-start.10 = (f32[8,12288]{1,0:T(8,128)S(1)}, f32[8,12288]{1,0:T(8,128)S(1)}, u32[]{:S(2)}, u32[]{:S(2)}) collective-permute-start(f32[8,12288]{1,0:T(8,128)S(1)} %get-tuple-element.119), channel_id=1, source_target_pairs={{0,30},{6,36},{12,42},{18,48},{24,54},{30,60},{36,66},{42,72},{48,... | collective-permute-start | bytes 1179656 | tf_op jit(solution)/shard_map/ppermute | solution.py:12
  139.5 100.1 %collective-permute-start.9 = (f32[8,12288]{1,0:T(8,128)S(1)}, f32[8,12288]{1,0:T(8,128)S(1)}, u32[]{:S(2)}, u32[]{:S(2)}) collective-permute-start(f32[8,12288]{1,0:T(8,128)S(1)} %get-tuple-element.120), channel_id=1, source_target_pairs={{0,24},{6,30},{12,36},{18,42},{24,48},{30,54},{36,60},{42,66},{48,... | collective-permute-start | bytes 1179656 | tf_op jit(solution)/shard_map/ppermute | solution.py:12
  144.0 95.6 %collective-permute-start.8 = (f32[8,12288]{1,0:T(8,128)S(1)}, f32[8,12288]{1,0:T(8,128)S(1)}, u32[]{:S(2)}, u32[]{:S(2)}) collective-permute-start(f32[8,12288]{1,0:T(8,128)S(1)} %get-tuple-element.121), channel_id=1, source_target_pairs={{0,18},{6,24},{12,30},{18,36},{24,42},{30,48},{36,54},{42,60},{48,... | collective-permute-start | bytes 1179656 | tf_op jit(solution)/shard_map/ppermute | solution.py:12
  146.7 128.6 %collective-permute-start.7 = (f32[8,12288]{1,0:T(8,128)S(1)}, f32[8,12288]{1,0:T(8,128)S(1)}, u32[]{:S(2)}, u32[]{:S(2)}) collective-permute-start(f32[8,12288]{1,0:T(8,128)S(1)} %get-tuple-element.122), channel_id=1, source_target_pairs={{0,12},{6,18},{12,24},{18,30},{24,36},{30,42},{36,48},{42,54},{48,... | collective-permute-start | bytes 1179656 | tf_op jit(solution)/shard_map/ppermute | solution.py:12
Sparse Core Ops, SparseCore 0:
  9.7 71.4 all-gather.1
  110.4 136.4 reduce-scatter.1
where the time goes:
time: 285 us; the launch traced here: 284 us
  starting transfers between devices  133 us (47%)
  waiting for transfers between devices  111 us (39%)
  between operations  14.3 us (5%)
  other arithmetic  13.3 us (5%)
  local copies, waits for them, and re-layouts  11 us (4%)
    ppermute x12, starting transfers between devices, from_behind(): return lax.ppermute(value, axis, pairs)  133 us
    ppermute x12, waiting for transfers between devices, from_behind(): return lax.ppermute(value, axis, pairs)  111 us
  transfers between devices with their start and end apart: 14, of which 4 were waited for; matrix products, arithmetic and copies ran while one was open for 1% of the time, Pallas kernels for 0%

commit v1 on v0

v1 whole, which is shorter than its diff:
```python
import functools

import jax
import jax.numpy as jnp
from jax import lax
from jax.experimental import pallas as pl
from jax.experimental.pallas import tpu as pltpu
from jax.sharding import PartitionSpec as P

AXES = ("row", "col")
VMEM_BYTES = 40 * 1024 * 1024
LIST_TAIL = 16


def whole(count):
    return [pl.BlockSpec(memory_space=pltpu.VMEM)] * count


def send(value, moves):
    return lax.ppermute(value, AXES, moves)


def moves_of(rows, cols, target):
    pairs = []
    for row in range(rows):
        for col in range(cols):
            to = target(row, col)
            if to is not None and 0 <= to[0] < rows:
                pairs.append((row * cols + col, to[0] * cols + to[1]))
    return pairs


def across_columns(value, rows, cols):
    half = cols // 2
    far = send(value, moves_of(rows, cols, lambda r, c: (r, (c + half) % cols)))
    pair = jnp.concatenate([value, far], axis=0)
    parts = [pair]
    for step in (1, 2):
        parts.append(
            send(pair, moves_of(rows, cols, lambda r, c, s=step: (r, c // half * half + (c % half + s) % half)))
        )
    return parts


def along_rows(value, rows, cols, way):
    last_half = 1 if way < 0 else 0
    across = send(value, moves_of(rows, cols, lambda r, c: (r ^ 2, c)))
    both = jnp.concatenate([value, across], axis=0)
    next_group = send(both, moves_of(rows, cols, lambda r, c: (r + 4 * way, c)))
    far_group = send(
        across,
        moves_of(rows, cols, lambda r, c: (r + 8 * way, c) if r // 2 % 2 == last_half else None),
    )
    here = jnp.concatenate([both, next_group, far_group], axis=0)
    there = send(here, moves_of(rows, cols, lambda r, c: (r ^ 1, c)))
    return [here, there]


def product_kernel(forward, parts, places_ref, counts_ref, *refs):
    pieces, (tiles_ref, tail_ref, out_ref, wide, sums) = refs[:parts], refs[parts:]
    start = 0
    for piece in pieces:
        wide[start : start + piece.shape[0], :] = piece[...].astype(jnp.float32)
        start += piece.shape[0]
    slots = tiles_ref.shape[0]
    lanes = lax.broadcasted_iota(jnp.int32, (8, 128), 1)
    for slot in range(slots):
        place = pl.multiple_of(places_ref[slot] * 8, 8)
        mask = lanes < counts_ref[slot]
        x = wide[pl.ds(place, 8), :]
        if forward:
            y = lax.dot_general(
                x.astype(jnp.bfloat16), tiles_ref[slot], (((1,), (1,)), ((), ())), preferred_element_type=jnp.float32
            )
            y = jnp.where(mask, y, 0.0)
        else:
            x = jnp.where(mask, x, 0.0).astype(jnp.bfloat16)
            y = lax.dot_general(x, tiles_ref[slot], (((1,), (0,)), ((), ())), preferred_element_type=jnp.float32)
        sums[pl.ds(slot, 8, stride=slots), :] = y
    out_ref[: 8 * slots, :] = sums[...].astype(jnp.bfloat16)
    out_ref[8 * slots :, :] = tail_ref[...]


def products(forward, parts, places, counts, tiles, tail):
    slots = tiles.shape[0]
    total = sum(p.shape[0] for p in parts)
    return pl.pallas_call(
        functools.partial(product_kernel, forward, len(parts)),
        out_shape=jax.ShapeDtypeStruct((8 * slots + LIST_TAIL, 128), jnp.bfloat16),
        in_specs=[pl.BlockSpec(memory_space=pltpu.SMEM)] * 2 + whole(len(parts) + 2),
        out_specs=pl.BlockSpec(memory_space=pltpu.VMEM),
        scratch_shapes=[pltpu.VMEM((total, 128), jnp.float32), pltpu.VMEM((8 * slots, 128), jnp.float32)],
        compiler_params=pltpu.CompilerParams(vmem_limit_bytes=VMEM_BYTES),
        cost_estimate=pl.CostEstimate(flops=2 * 8 * 128 * 128 * slots, bytes_accessed=total * 256 + 2 * 2**20, transcendentals=0),
    )(places, counts, *parts, tiles, tail)


def sum_kernel(parts, slots, base_ref, *refs):
    lists, (out_ref, acc) = refs[:parts], refs[parts:]
    tiles_here = out_ref.shape[0] // 8
    rows = 8 * slots + LIST_TAIL
    own = lax.broadcasted_iota(jnp.int32, (tiles_here, 128), 0) + base_ref[0]
    own = own.astype(jnp.float32)
    acc[...] = jnp.zeros_like(acc)
    for part in lists:
        for start in range(0, part.shape[0], rows):
            digits = part[start + 8 * slots : start + rows, :].astype(jnp.float32)
            ids = digits[0:1] + 64.0 * digits[1:2] + 4096.0 * digits[2:3]
            chosen = jnp.where(own == ids, 1.0, 0.0)[:, :slots].astype(jnp.bfloat16)
            for vec in range(8):
                values = part[start + vec * slots : start + (vec + 1) * slots, :]
                acc[vec] += jnp.dot(chosen, values, preferred_element_type=jnp.float32)
    for vec in range(8):
        out_ref[pl.ds(vec, tiles_here, stride=8), :] = acc[vec]


def summed(lists, slots, base, tiles_here):
    return pl.pallas_call(
        functools.partial(sum_kernel, len(lists), slots),
        out_shape=jax.ShapeDtypeStruct((8 * tiles_here, 128), jnp.float32),
        in_specs=[pl.BlockSpec(memory_space=pltpu.SMEM)] + whole(len(lists)),
        out_specs=pl.BlockSpec(memory_space=pltpu.VMEM),
        scratch_shapes=[pltpu.VMEM((8, tiles_here, 128), jnp.float32)],
        compiler_params=pltpu.CompilerParams(vmem_limit_bytes=VMEM_BYTES),
    )(base, *lists)


def tail_of(ids):
    digits = jnp.stack([jnp.where(ids < 0, ids, ids % 64), jnp.maximum(ids, 0) // 64 % 64, jnp.maximum(ids, 0) // 4096])
    return jnp.pad(digits.astype(jnp.bfloat16), ((0, LIST_TAIL - 3), (0, 128 - ids.shape[0])))


def local(vectors, tiles, tile_rows, tile_cols, row_counts, live_tiles):
    vec_count, seg_len = vectors.shape
    slots, tile_len = tiles.shape[:2]
    rows, cols = lax.axis_size("row"), lax.axis_size("col")
    half = cols // 2
    per_piece = seg_len // tile_len
    band = cols * per_piece
    row, col = lax.axis_index("row"), lax.axis_index("col")

    live = jnp.arange(slots, dtype=jnp.int32) < live_tiles[0]
    counts = jnp.where(live, row_counts, 0)
    row_piece = tile_rows // per_piece % cols
    row_part = (col % half - row_piece % half) % half * 2 + jnp.where(row_piece // half != col // half, 1, 0)
    row_places = row_part * per_piece + tile_rows % per_piece
    col_row = tile_cols // band
    group = col_row // 4 - row // 4
    other = (col_row % 4) ^ (row % 4)
    col_part = (other & 1) * 5 + jnp.where(group == 2, 4, (other >> 1) + 2 * group)
    col_places = col_part * per_piece + tile_cols % per_piece

    def flat(x):
        return x.reshape(vec_count, per_piece, tile_len).transpose(1, 0, 2).reshape(-1, tile_len)

    rounded = flat(vectors.astype(jnp.bfloat16))
    row_parts = across_columns(rounded, rows, cols)
    col_parts = along_rows(rounded, rows, cols, -1)
    mirror = products(False, row_parts, row_places, counts, tiles, tail_of(jnp.where(live, tile_cols, -1)))
    forward = products(True, col_parts, col_places, counts, tiles, tail_of(jnp.where(live, tile_rows, -1)))
    mirror_lists = along_rows(mirror, rows, cols, 1)
    forward_lists = across_columns(forward, rows, cols)
    base = ((row * cols + col) * per_piece).reshape(1)
    total = summed(mirror_lists + forward_lists, slots, base, per_piece)
    return total.reshape(per_piece, vec_count, tile_len).transpose(1, 0, 2).reshape(vec_count, seg_len)


def solution(mesh):
    placed = (
        P(None, AXES),
        P(AXES, None, None),
        P(AXES),
        P(AXES),
        P(AXES),
        P(AXES),
    )
    return jax.shard_map(local, mesh=mesh, in_specs=placed, out_specs=P(None, AXES), check_vma=False)
```

time: 285 us -> 138 us (0.48)
  the two profiles are of different devices: /device:TPU:155 before, /device:TPU:7 now
where the time goes in v1:
time: 138 us; the launch traced here: 137 us
  starting transfers between devices  64.4 us (47%)
  waiting for transfers between devices  63.3 us (46%)
  Pallas kernels  5.14 us (4%)
  other arithmetic  2.01 us (1%)
  local copies, waits for them, and re-layouts  1.6 us (1%)
    ppermute x14, starting transfers between devices, send(): return lax.ppermute(value, AXES, moves)  64.4 us
    ppermute x14, waiting for transfers between devices, send(): return lax.ppermute(value, AXES, moves)  63.3 us
    pallas_call x2, Pallas kernels, products(): pl.pallas_call(functools.partial(product_kernel, forward, len(parts)), ou...  3.41 us
  transfers between devices with their start and end apart: 14, of which 7 were waited for; matrix products, arithmetic and copies ran while one was open for 1% of the time, Pallas kernels for 2%

profile of v1, /device:TPU:7, one launch (start us, length us, event | category | flops | bytes accessed | tf_op | source)
XLA Modules:
  0.0 137.4 jit_solution(7952777758238673304)
XLA Ops:
  1.1 14.9 %collective-permute-start.7 = (bf16[768,128]{1,0:T(8,128)(2,1)S(1)}, bf16[768,128]{1,0:T(8,128)(2,1)S(1)}, u32[]{:S(2)}, u32[]{:S(2)}) collective-permute-start(bf16[768,128]{1,0:T(8,128)(2,1)S(1)} %convert_bitcast_fusion), channel_id=1, source_target_pairs={{0,12},{1,13},{2,14},{3,15},{4,16},{5,17},{6,18},{7,19},{8,20},{9,... | collective-permute-start | bytes 589832 | tf_op jit(solution)/shard_map/ppermute | solution.py:20
  15.9 4.9 %collective-permute-start = (bf16[768,128]{1,0:T(8,128)(2,1)S(1)}, bf16[768,128]{1,0:T(8,128)(2,1)S(1)}, u32[]{:S(2)}, u32[]{:S(2)}) collective-permute-start(bf16[768,128]{1,0:T(8,128)(2,1)S(1)} %convert_bitcast_fusion), channel_id=1, source_target_pairs={{0,3},{1,4},{2,5},{3,0},{4,1},{5,2},{6,9},{7,10},{8,11},{9,6},{10,... | collective-permute-start | bytes 589832 | tf_op jit(solution)/shard_map/ppermute | solution.py:20
  22.3 20.1 %collective-permute-done = bf16[768,128]{1,0:T(8,128)(2,1)S(1)} collective-permute-done((bf16[768,128]{1,0:T(8,128)(2,1)S(1)}, bf16[768,128]{1,0:T(8,128)(2,1)S(1)}, u32[]{:S(2)}, u32[]{:S(2)}) %collective-permute-start) | collective-permute-done | bytes 196640 | tf_op jit(solution)/shard_map/ppermute | solution.py:20
  42.4 1.9 %collective-permute-start.1 = (bf16[1536,128]{1,0:T(8,128)(2,1)S(1)}, bf16[1536,128]{1,0:T(8,128)(2,1)S(1)}, u32[]{:S(2)}, u32[]{:S(2)}) collective-permute-start(bf16[1536,128]{1,0:T(8,128)(2,1)S(1)} %get-tuple-element.6.refs_0_), channel_id=1, source_target_pairs={{0,1},{1,2},{2,0},{3,4},{4,5},{5,3},{6,7},{7,8},{8,6},{9,10},{10,1... | collective-permute-start | bytes 1179656 | tf_op jit(solution)/shard_map/ppermute | solution.py:20
  44.4 4.3 %collective-permute-start.2 = (bf16[1536,128]{1,0:T(8,128)(2,1)S(1)}, bf16[1536,128]{1,0:T(8,128)(2,1)S(1)}, u32[]{:S(2)}, u32[]{:S(2)}) collective-permute-start(bf16[1536,128]{1,0:T(8,128)(2,1)S(1)} %get-tuple-element.6.refs_0_), channel_id=1, source_target_pairs={{0,2},{1,0},{2,1},{3,5},{4,3},{5,4},{6,8},{7,6},{8,7},{9,11},{10,9... | collective-permute-start | bytes 1179656 | tf_op jit(solution)/shard_map/ppermute | solution.py:20
  48.6 5.4 %collective-permute-start.8 = (bf16[1536,128]{1,0:T(8,128)(2,1)S(1)}, bf16[1536,128]{1,0:T(8,128)(2,1)S(1)}, u32[]{:S(2)}, u32[]{:S(2)}) collective-permute-start(bf16[1536,128]{1,0:T(8,128)(2,1)S(1)} %get-tuple-element.5), channel_id=1, source_target_pairs={{24,0},{25,1},{26,2},{27,3},{28,4},{29,5},{30,6},{31,7},{32,8},{33... | collective-permute-start | bytes 1179656 | tf_op jit(solution)/shard_map/ppermute | solution.py:20
  54.8 9.9 %collective-permute-done.2.refs_2_ = bf16[1536,128]{1,0:T(8,128)(2,1)S(1)} collective-permute-done((bf16[1536,128]{1,0:T(8,128)(2,1)S(1)}, bf16[1536,128]{1,0:T(8,128)(2,1)S(1)}, u32[]{:S(2)}, u32[]{:S(2)}) %collective-permute-start.2) | collective-permute-done | bytes 393248 | tf_op jit(solution)/shard_map/ppermute | solution.py:20
  64.7 1.6 %copy-done = bf16[64,128,128]{2,1,0:T(8,128)(2,1)S(1)} copy-done((bf16[64,128,128]{2,1,0:T(8,128)(2,1)S(1)}, bf16[64,128,128]{2,1,0:T(8,128)(2,1)}, u32[]{:S(2)}) %copy-start) | copy-done | bytes 2097176
  66.3 1.4 %shard_map.64 = bf16[528,128]{1,0:T(8,128)(2,1)S(1)} custom-call(s32[64]{0:T(128)S(1)} %get-tuple-element.10.places_ref, s32[64]{0:T(128)S(1)} %fusion.39.counts_ref, bf16[1536,128]{1,0:T(8,128)(2,1)S(1)} %get-tuple-element.6.refs_0_, bf16[1536,128]{1,0:T(8,128)(2,1)S(1)} %collective-permute-done.1.refs_1_, ...), custom_call_target="tpu_custom_call" | custom-call | flops 16777216 | bytes 3276800 | tf_op jit(solution)/shard_map/pallas_call | solution.py:87
  67.7 5.7 %collective-permute-start.3 = (bf16[528,128]{1,0:T(8,128)(2,1)S(1)}, bf16[528,128]{1,0:T(8,128)(2,1)S(1)}, u32[]{:S(2)}, u32[]{:S(2)}) collective-permute-start(bf16[528,128]{1,0:T(8,128)(2,1)S(1)} %shard_map.64), channel_id=1, source_target_pairs={{0,12},{1,13},{2,14},{3,15},{4,16},{5,17},{6,18},{7,19},{8,20},{9,... | collective-permute-start | bytes 405512 | tf_op jit(solution)/shard_map/ppermute | solution.py:20
  73.5 2.9 %collective-permute-start.10 = (bf16[3840,128]{1,0:T(8,128)(2,1)S(1)}, bf16[3840,128]{1,0:T(8,128)(2,1)S(1)}, u32[]{:S(2)}, u32[]{:S(2)}) collective-permute-start(bf16[3840,128]{1,0:T(8,128)(2,1)S(1)} %pad_maximum_fusion.refs_0_), channel_id=1, source_target_pairs={{0,6},{1,7},{2,8},{3,9},{4,10},{5,11},{6,0},{7,1},{8,2},{9,3},{10,... | collective-permute-start | bytes 2949128 | tf_op jit(solution)/shard_map/ppermute | solution.py:20
  76.4 8.1 %collective-permute-done.3 = bf16[528,128]{1,0:T(8,128)(2,1)S(1)} collective-permute-done((bf16[528,128]{1,0:T(8,128)(2,1)S(1)}, bf16[528,128]{1,0:T(8,128)(2,1)S(1)}, u32[]{:S(2)}, u32[]{:S(2)}) %collective-permute-start.3) | collective-permute-done | bytes 135200 | tf_op jit(solution)/shard_map/ppermute | solution.py:20
  84.5 3.2 %collective-permute-start.4 = (bf16[1056,128]{1,0:T(8,128)(2,1)S(1)}, bf16[1056,128]{1,0:T(8,128)(2,1)S(1)}, u32[]{:S(2)}, u32[]{:S(2)}) collective-permute-start(bf16[1056,128]{1,0:T(8,128)(2,1)S(1)} %pad_maximum_fusion.4), channel_id=1, source_target_pairs={{0,24},{1,25},{2,26},{3,27},{4,28},{5,29},{6,30},{7,31},{8,32},{9,... | collective-permute-start | bytes 811016 | tf_op jit(solution)/shard_map/ppermute | solution.py:20
  87.8 4.2 %collective-permute-start.5 = (bf16[528,128]{1,0:T(8,128)(2,1)S(1)}, bf16[528,128]{1,0:T(8,128)(2,1)S(1)}, u32[]{:S(2)}, u32[]{:S(2)}) collective-permute-start(bf16[528,128]{1,0:T(8,128)(2,1)S(1)} %collective-permute-done.3), channel_id=1, source_target_pairs={{0,48},{1,49},{2,50},{3,51},{4,52},{5,53},{6,54},{7,55},{8,56},{9,... | collective-permute-start | bytes 405512 | tf_op jit(solution)/shard_map/ppermute | solution.py:20
  92.0 9.0 %collective-permute-done.5 = bf16[528,128]{1,0:T(8,128)(2,1)S(1)} collective-permute-done((bf16[528,128]{1,0:T(8,128)(2,1)S(1)}, bf16[528,128]{1,0:T(8,128)(2,1)S(1)}, u32[]{:S(2)}, u32[]{:S(2)}) %collective-permute-start.5) | collective-permute-done | bytes 135200 | tf_op jit(solution)/shard_map/ppermute | solution.py:20
  101.0 3.3 %collective-permute-start.6 = (bf16[2640,128]{1,0:T(8,128)(2,1)S(1)}, bf16[2640,128]{1,0:T(8,128)(2,1)S(1)}, u32[]{:S(2)}, u32[]{:S(2)}) collective-permute-start(bf16[2640,128]{1,0:T(8,128)(2,1)S(1)} %pad_maximum_fusion.1.refs_0_), channel_id=1, source_target_pairs={{0,6},{1,7},{2,8},{3,9},{4,10},{5,11},{6,0},{7,1},{8,2},{9,3},{10,... | collective-permute-start | bytes 2027528 | tf_op jit(solution)/shard_map/ppermute | solution.py:20
  104.3 2.0 %shard_map.65 = bf16[528,128]{1,0:T(8,128)(2,1)S(1)} custom-call(s32[64]{0:T(128)S(1)} %get-tuple-element.11.places_ref, s32[64]{0:T(128)S(1)} %fusion.39.counts_ref, bf16[3840,128]{1,0:T(8,128)(2,1)S(1)} %pad_maximum_fusion.refs_0_, bf16[3840,128]{1,0:T(8,128)(2,1)S(1)} %collective-permute-done.10.refs_1_, bf16[64,128,128]{2,1,0:T(8,128)(2,1)S(1)} %copy-done.1, ...), custom_call_target="tpu_custom_call" | custom-call | flops 16777216 | bytes 4063232 | tf_op jit(solution)/shard_map/pallas_call | solution.py:87
  106.4 7.0 %collective-permute-start.11 = (bf16[528,128]{1,0:T(8,128)(2,1)S(1)}, bf16[528,128]{1,0:T(8,128)(2,1)S(1)}, u32[]{:S(2)}, u32[]{:S(2)}) collective-permute-start(bf16[528,128]{1,0:T(8,128)(2,1)S(1)} %shard_map.65), channel_id=1, source_target_pairs={{0,3},{1,4},{2,5},{3,0},{4,1},{5,2},{6,9},{7,10},{8,11},{9,6},{10,... | collective-permute-start | bytes 405512 | tf_op jit(solution)/shard_map/ppermute | solution.py:20
  113.3 5.3 %collective-permute-done.11 = bf16[528,128]{1,0:T(8,128)(2,1)S(1)} collective-permute-done((bf16[528,128]{1,0:T(8,128)(2,1)S(1)}, bf16[528,128]{1,0:T(8,128)(2,1)S(1)}, u32[]{:S(2)}, u32[]{:S(2)}) %collective-permute-start.11) | collective-permute-done | bytes 135200 | tf_op jit(solution)/shard_map/ppermute | solution.py:20
  118.7 1.9 %collective-permute-start.12 = (bf16[1056,128]{1,0:T(8,128)(2,1)S(1)}, bf16[1056,128]{1,0:T(8,128)(2,1)S(1)}, u32[]{:S(2)}, u32[]{:S(2)}) collective-permute-start(bf16[1056,128]{1,0:T(8,128)(2,1)S(1)} %pad_maximum_fusion.5.refs_2_), channel_id=1, source_target_pairs={{0,1},{1,2},{2,0},{3,4},{4,5},{5,3},{6,7},{7,8},{8,6},{9,10},{10,1... | collective-permute-start | bytes 811016 | tf_op jit(solution)/shard_map/ppermute | solution.py:20
  120.6 4.3 %collective-permute-start.13 = (bf16[1056,128]{1,0:T(8,128)(2,1)S(1)}, bf16[1056,128]{1,0:T(8,128)(2,1)S(1)}, u32[]{:S(2)}, u32[]{:S(2)}) collective-permute-start(bf16[1056,128]{1,0:T(8,128)(2,1)S(1)} %pad_maximum_fusion.5.refs_2_), channel_id=1, source_target_pairs={{0,2},{1,0},{2,1},{3,5},{4,3},{5,4},{6,8},{7,6},{8,7},{9,11},{10,9... | collective-permute-start | bytes 811016 | tf_op jit(solution)/shard_map/ppermute | solution.py:20
  124.9 4.3 %collective-permute-done.12.refs_3_ = bf16[1056,128]{1,0:T(8,128)(2,1)S(1)} collective-permute-done((bf16[1056,128]{1,0:T(8,128)(2,1)S(1)}, bf16[1056,128]{1,0:T(8,128)(2,1)S(1)}, u32[]{:S(2)}, u32[]{:S(2)}) %collective-permute-start.12) | collective-permute-done | bytes 270368 | tf_op jit(solution)/shard_map/ppermute | solution.py:20
  129.2 6.5 %collective-permute-done.13.refs_4_ = bf16[1056,128]{1,0:T(8,128)(2,1)S(1)} collective-permute-done((bf16[1056,128]{1,0:T(8,128)(2,1)S(1)}, bf16[1056,128]{1,0:T(8,128)(2,1)S(1)}, u32[]{:S(2)}, u32[]{:S(2)}) %collective-permute-start.13) | collective-permute-done | bytes 270368 | tf_op jit(solution)/shard_map/ppermute | solution.py:20
  135.7 1.7 %shard_map.66 = f32[768,128]{1,0:T(8,128)} custom-call(s32[1]{0:T(128)} %bitcast.base_ref, bf16[2640,128]{1,0:T(8,128)(2,1)S(1)} %pad_maximum_fusion.1.refs_0_, bf16[2640,128]{1,0:T(8,128)(2,1)S(1)} %collective-permute-done.6.refs_1_, bf16[1056,128]{1,0:T(8,128)(2,1)S(1)} %pad_maximum_fusion.5.refs_2_, ...), custom_call_target="tpu_custom_call" | custom-call | tf_op jit(solution)/shard_map/pallas_call | solution.py:118
  (26 shorter events, 2.7 us)
Async XLA Ops:
  0.0 54.0 %copy-start.2 = (s32[64]{0:T(128)S(1)}, s32[64]{0:T(128)}, u32[]{:S(2)}) copy-start(s32[64]{0:T(128)} %param.9) | copy-start | bytes 772
  0.0 54.8 %copy-start.3 = (s32[64]{0:T(128)S(1)}, s32[64]{0:T(128)}, u32[]{:S(2)}) copy-start(s32[64]{0:T(128)} %param.10) | copy-start | bytes 772
  1.1 21.2 %collective-permute-start.7 = (bf16[768,128]{1,0:T(8,128)(2,1)S(1)}, bf16[768,128]{1,0:T(8,128)(2,1)S(1)}, u32[]{:S(2)}, u32[]{:S(2)}) collective-permute-start(bf16[768,128]{1,0:T(8,128)(2,1)S(1)} %convert_bitcast_fusion), channel_id=1, source_target_pairs={{0,12},{1,13},{2,14},{3,15},{4,16},{5,17},{6,18},{7,19},{8,20},{9,... | collective-permute-start | bytes 589832 | tf_op jit(solution)/shard_map/ppermute | solution.py:20
  15.9 26.5 %collective-permute-start = (bf16[768,128]{1,0:T(8,128)(2,1)S(1)}, bf16[768,128]{1,0:T(8,128)(2,1)S(1)}, u32[]{:S(2)}, u32[]{:S(2)}) collective-permute-start(bf16[768,128]{1,0:T(8,128)(2,1)S(1)} %convert_bitcast_fusion), channel_id=1, source_target_pairs={{0,3},{1,4},{2,5},{3,0},{4,1},{5,2},{6,9},{7,10},{8,11},{9,6},{10,... | collective-permute-start | bytes 589832 | tf_op jit(solution)/shard_map/ppermute | solution.py:20
  42.4 12.3 %collective-permute-start.1 = (bf16[1536,128]{1,0:T(8,128)(2,1)S(1)}, bf16[1536,128]{1,0:T(8,128)(2,1)S(1)}, u32[]{:S(2)}, u32[]{:S(2)}) collective-permute-start(bf16[1536,128]{1,0:T(8,128)(2,1)S(1)} %get-tuple-element.6.refs_0_), channel_id=1, source_target_pairs={{0,1},{1,2},{2,0},{3,4},{4,5},{5,3},{6,7},{7,8},{8,6},{9,10},{10,1... | collective-permute-start | bytes 1179656 | tf_op jit(solution)/shard_map/ppermute | solution.py:20
  44.4 20.3 %collective-permute-start.2 = (bf16[1536,128]{1,0:T(8,128)(2,1)S(1)}, bf16[1536,128]{1,0:T(8,128)(2,1)S(1)}, u32[]{:S(2)}, u32[]{:S(2)}) collective-permute-start(bf16[1536,128]{1,0:T(8,128)(2,1)S(1)} %get-tuple-element.6.refs_0_), channel_id=1, source_target_pairs={{0,2},{1,0},{2,1},{3,5},{4,3},{5,4},{6,8},{7,6},{8,7},{9,11},{10,9... | collective-permute-start | bytes 1179656 | tf_op jit(solution)/shard_map/ppermute | solution.py:20
  48.6 24.8 %collective-permute-start.8 = (bf16[1536,128]{1,0:T(8,128)(2,1)S(1)}, bf16[1536,128]{1,0:T(8,128)(2,1)S(1)}, u32[]{:S(2)}, u32[]{:S(2)}) collective-permute-start(bf16[1536,128]{1,0:T(8,128)(2,1)S(1)} %get-tuple-element.5), channel_id=1, source_target_pairs={{24,0},{25,1},{26,2},{27,3},{28,4},{29,5},{30,6},{31,7},{32,8},{33... | collective-permute-start | bytes 1179656 | tf_op jit(solution)/shard_map/ppermute | solution.py:20
  54.1 19.3 %collective-permute-start.9 = (bf16[768,128]{1,0:T(8,128)(2,1)S(1)}, bf16[768,128]{1,0:T(8,128)(2,1)S(1)}, u32[]{:S(2)}, u32[]{:S(2)}) collective-permute-start(bf16[768,128]{1,0:T(8,128)(2,1)S(1)} %collective-permute-done.7), channel_id=1, source_target_pairs={{60,12},{61,13},{62,14},{63,15},{64,16},{65,17},{66,18},{67,19},{6... | collective-permute-start | bytes 589832 | tf_op jit(solution)/shard_map/ppermute | solution.py:20
  64.7 1.6 %copy-start = (bf16[64,128,128]{2,1,0:T(8,128)(2,1)S(1)}, bf16[64,128,128]{2,1,0:T(8,128)(2,1)}, u32[]{:S(2)}) copy-start(bf16[64,128,128]{2,1,0:T(8,128)(2,1)} %refs_2_.1) | copy-start | bytes 6291460
  67.7 36.6 %copy-start.1 = (bf16[64,128,128]{2,1,0:T(8,128)(2,1)S(1)}, bf16[64,128,128]{2,1,0:T(8,128)(2,1)}, u32[]{:S(2)}) copy-start(bf16[64,128,128]{2,1,0:T(8,128)(2,1)} %refs_2_.1) | copy-start | bytes 6291460
  67.7 16.8 %collective-permute-start.3 = (bf16[528,128]{1,0:T(8,128)(2,1)S(1)}, bf16[528,128]{1,0:T(8,128)(2,1)S(1)}, u32[]{:S(2)}, u32[]{:S(2)}) collective-permute-start(bf16[528,128]{1,0:T(8,128)(2,1)S(1)} %shard_map.64), channel_id=1, source_target_pairs={{0,12},{1,13},{2,14},{3,15},{4,16},{5,17},{6,18},{7,19},{8,20},{9,... | collective-permute-start | bytes 405512 | tf_op jit(solution)/shard_map/ppermute | solution.py:20
  73.5 30.8 %collective-permute-start.10 = (bf16[3840,128]{1,0:T(8,128)(2,1)S(1)}, bf16[3840,128]{1,0:T(8,128)(2,1)S(1)}, u32[]{:S(2)}, u32[]{:S(2)}) collective-permute-start(bf16[3840,128]{1,0:T(8,128)(2,1)S(1)} %pad_maximum_fusion.refs_0_), channel_id=1, source_target_pairs={{0,6},{1,7},{2,8},{3,9},{4,10},{5,11},{6,0},{7,1},{8,2},{9,3},{10,... | collective-permute-start | bytes 2949128 | tf_op jit(solution)/shard_map/ppermute | solution.py:20
  84.5 16.4 %collective-permute-start.4 = (bf16[1056,128]{1,0:T(8,128)(2,1)S(1)}, bf16[1056,128]{1,0:T(8,128)(2,1)S(1)}, u32[]{:S(2)}, u32[]{:S(2)}) collective-permute-start(bf16[1056,128]{1,0:T(8,128)(2,1)S(1)} %pad_maximum_fusion.4), channel_id=1, source_target_pairs={{0,24},{1,25},{2,26},{3,27},{4,28},{5,29},{6,30},{7,31},{8,32},{9,... | collective-permute-start | bytes 811016 | tf_op jit(solution)/shard_map/ppermute | solution.py:20
  87.8 13.2 %collective-permute-start.5 = (bf16[528,128]{1,0:T(8,128)(2,1)S(1)}, bf16[528,128]{1,0:T(8,128)(2,1)S(1)}, u32[]{:S(2)}, u32[]{:S(2)}) collective-permute-start(bf16[528,128]{1,0:T(8,128)(2,1)S(1)} %collective-permute-done.3), channel_id=1, source_target_pairs={{0,48},{1,49},{2,50},{3,51},{4,52},{5,53},{6,54},{7,55},{8,56},{9,... | collective-permute-start | bytes 405512 | tf_op jit(solution)/shard_map/ppermute | solution.py:20
  101.0 23.9 %collective-permute-start.6 = (bf16[2640,128]{1,0:T(8,128)(2,1)S(1)}, bf16[2640,128]{1,0:T(8,128)(2,1)S(1)}, u32[]{:S(2)}, u32[]{:S(2)}) collective-permute-start(bf16[2640,128]{1,0:T(8,128)(2,1)S(1)} %pad_maximum_fusion.1.refs_0_), channel_id=1, source_target_pairs={{0,6},{1,7},{2,8},{3,9},{4,10},{5,11},{6,0},{7,1},{8,2},{9,3},{10,... | collective-permute-start | bytes 2027528 | tf_op jit(solution)/shard_map/ppermute | solution.py:20
  106.4 12.3 %collective-permute-start.11 = (bf16[528,128]{1,0:T(8,128)(2,1)S(1)}, bf16[528,128]{1,0:T(8,128)(2,1)S(1)}, u32[]{:S(2)}, u32[]{:S(2)}) collective-permute-start(bf16[528,128]{1,0:T(8,128)(2,1)S(1)} %shard_map.65), channel_id=1, source_target_pairs={{0,3},{1,4},{2,5},{3,0},{4,1},{5,2},{6,9},{7,10},{8,11},{9,6},{10,... | collective-permute-start | bytes 405512 | tf_op jit(solution)/shard_map/ppermute | solution.py:20
  118.7 10.5 %collective-permute-start.12 = (bf16[1056,128]{1,0:T(8,128)(2,1)S(1)}, bf16[1056,128]{1,0:T(8,128)(2,1)S(1)}, u32[]{:S(2)}, u32[]{:S(2)}) collective-permute-start(bf16[1056,128]{1,0:T(8,128)(2,1)S(1)} %pad_maximum_fusion.5.refs_2_), channel_id=1, source_target_pairs={{0,1},{1,2},{2,0},{3,4},{4,5},{5,3},{6,7},{7,8},{8,6},{9,10},{10,1... | collective-permute-start | bytes 811016 | tf_op jit(solution)/shard_map/ppermute | solution.py:20
  120.6 15.1 %collective-permute-start.13 = (bf16[1056,128]{1,0:T(8,128)(2,1)S(1)}, bf16[1056,128]{1,0:T(8,128)(2,1)S(1)}, u32[]{:S(2)}, u32[]{:S(2)}) collective-permute-start(bf16[1056,128]{1,0:T(8,128)(2,1)S(1)} %pad_maximum_fusion.5.refs_2_), channel_id=1, source_target_pairs={{0,2},{1,0},{2,1},{3,5},{4,3},{5,4},{6,8},{7,6},{8,7},{9,11},{10,9... | collective-permute-start | bytes 811016 | tf_op jit(solution)/shard_map/ppermute | solution.py:20

commit v2 on v1

v2 whole, which is shorter than its diff:
```python
import functools

import jax
import jax.numpy as jnp
from jax import lax
from jax.experimental import pallas as pl
from jax.experimental.pallas import tpu as pltpu
from jax.sharding import PartitionSpec as P

AXES = ("row", "col")
VMEM_BYTES = 40 * 1024 * 1024
LIST_TAIL = 16
SHARE = 32
LANES = 128
VMEM = pl.BlockSpec(memory_space=pltpu.VMEM)
SMEM = pl.BlockSpec(memory_space=pltpu.SMEM)
PARAMS = pltpu.CompilerParams(vmem_limit_bytes=VMEM_BYTES)
LITTLE = pl.CostEstimate(flops=0, bytes_accessed=0, transcendentals=0)


def send(value, moves):
    return lax.ppermute(value, AXES, moves)


def moves_of(rows, cols, target):
    pairs = []
    for row in range(rows):
        for col in range(cols):
            to = target(row, col)
            if to is not None and 0 <= to[0] < rows:
                pairs.append((row * cols + col, to[0] * cols + to[1]))
    return pairs


def across_halves(value, rows, cols):
    return send(value, moves_of(rows, cols, lambda r, c: (r ^ 2, c)))


def next_groups(both, rows, cols, way):
    last_half = 1 if way < 0 else 0
    count = both.shape[0] // 2
    return [
        send(both, moves_of(rows, cols, lambda r, c: (r + 4 * way, c))),
        send(
            both[count:],
            moves_of(rows, cols, lambda r, c: (r + 8 * way, c) if r // 2 % 2 == last_half else None),
        ),
    ]


def other_core(here, rows, cols):
    return send(here, moves_of(rows, cols, lambda r, c: (r ^ 1, c)))


def over_columns(value, cols):
    return lax.all_to_all(value.reshape(cols, -1, LANES), "col", 0, 0).reshape(-1, LANES)


def after(value, *others):
    return lax.optimization_barrier((value, *others))[0]


def request_kernel(cols, per_piece, place_ref, rows_ref, live_ref, ids_ref, places_ref, used):
    slots = rows_ref.shape[0]
    me, start = place_ref[0], place_ref[1]
    for col in range(cols):
        used[col] = 0
    live = live_ref[0]
    for slot in range(slots):
        tile = rows_ref[slot] - start
        col = jnp.int32(0)
        for edge in range(1, cols):
            col = col + jnp.where(tile >= edge * per_piece, 1, 0)
        here = slot < live
        rank = used[col]
        used[col] = rank + jnp.where(here, 1, 0)
        ids_ref[col, 0, rank] = tile - col * per_piece
        late = jnp.where(rank < SHARE, 0, 1)
        chunk = jnp.where(col == me, 2 * cols + late, col + cols * late)
        places_ref[slot] = jnp.where(here, chunk * (8 * SHARE) + rank - late * SHARE, (2 * cols + 2) * 8 * SHARE)
    most = jnp.int32(0)
    for col in range(cols):
        most = jnp.maximum(most, jnp.where(col == me, 0, used[col]))
    for col in range(cols):
        ids_ref[col, 1, 0] = most
        ids_ref[col, 1, 1] = used[col]


def requests(place, tile_rows, live_tiles, cols, per_piece):
    slots = tile_rows.shape[0]
    return pl.pallas_call(
        functools.partial(request_kernel, cols, per_piece),
        out_shape=(
            jax.ShapeDtypeStruct((cols, 8, LANES), jnp.int32),
            jax.ShapeDtypeStruct((slots,), jnp.int32),
        ),
        in_specs=[SMEM, SMEM, SMEM],
        out_specs=(SMEM, SMEM),
        scratch_shapes=[pltpu.SMEM((cols,), jnp.int32)],
        cost_estimate=LITTLE,
    )(place, tile_rows, live_tiles)


def chosen_of(asked_ref, col, places):
    lanes = lax.broadcasted_iota(jnp.int32, places.shape, 1)
    asked = (places == asked_ref[col, 0:1, :]) & (lanes < asked_ref[col, 1:2, 1:2])
    return jnp.where(asked, 1.0, 0.0)


def reply_kernel(cols, slots, place_ref, asked_ref, x_ref, first_ref, second_ref, own_ref, wide):
    tiles = x_ref.shape[0] // 8
    wide[...] = x_ref[...].astype(jnp.float32)
    places = lax.broadcasted_iota(jnp.int32, (LANES, LANES), 0)
    wanted = [chosen_of(asked_ref, col, places).T[:slots, :tiles] for col in [*range(cols), place_ref[0]]]
    wanted = jnp.concatenate(wanted, axis=0).astype(jnp.bfloat16)
    for vec in range(8):
        x = wide[pl.ds(vec, tiles, stride=8), :].astype(jnp.bfloat16)
        found = jnp.dot(wanted, x, preferred_element_type=jnp.float32).astype(jnp.bfloat16)
        for col in range(cols + 1):
            early = found[col * slots : col * slots + SHARE]
            late = found[col * slots + SHARE : (col + 1) * slots]
            at = (col * 8 + vec) * SHARE
            if col < cols:
                first_ref[at : at + SHARE, :] = early
                second_ref[at : at + SHARE, :] = late
            else:
                own_ref[vec * SHARE : (vec + 1) * SHARE, :] = early
                own_ref[(8 + vec) * SHARE : (9 + vec) * SHARE, :] = late


def replies(place, asked, x, cols, slots):
    shape = jax.ShapeDtypeStruct((cols * 8 * SHARE, LANES), jnp.bfloat16)
    own = jax.ShapeDtypeStruct((2 * 8 * SHARE, LANES), jnp.bfloat16)
    return pl.pallas_call(
        functools.partial(reply_kernel, cols, slots),
        out_shape=(shape, shape, own),
        in_specs=[SMEM, VMEM, VMEM],
        out_specs=(VMEM, VMEM, VMEM),
        scratch_shapes=[pltpu.VMEM(x.shape, jnp.float32)],
        compiler_params=PARAMS,
        cost_estimate=LITTLE,
    )(place, asked, x)


def mirror_kernel(places_ref, counts_ref, first_ref, second_ref, own_ref, tiles_ref, tail_ref, out_ref, wide, sums):
    slots = tiles_ref.shape[0]
    part = first_ref.shape[0]
    wide[:part, :] = first_ref[...].astype(jnp.float32)
    wide[part : 2 * part, :] = second_ref[...].astype(jnp.float32)
    wide[2 * part : -8 * SHARE, :] = own_ref[...].astype(jnp.float32)
    wide[-8 * SHARE :, :] = jnp.zeros((8 * SHARE, LANES), jnp.float32)
    lanes = lax.broadcasted_iota(jnp.int32, (8, LANES), 1)
    for slot in range(slots):
        x = wide[pl.ds(places_ref[slot], 8, stride=SHARE), :]
        x = jnp.where(lanes < counts_ref[slot], x, 0.0).astype(jnp.bfloat16)
        y = lax.dot_general(x, tiles_ref[slot], (((1,), (0,)), ((), ())), preferred_element_type=jnp.float32)
        sums[pl.ds(slot, 8, stride=slots), :] = y
    out_ref[: 8 * slots, :] = sums[...].astype(jnp.bfloat16)
    out_ref[8 * slots :, :] = tail_ref[...]


def mirror_products(places, counts, first, second, own, tiles, tail):
    slots = tiles.shape[0]
    return pl.pallas_call(
        mirror_kernel,
        out_shape=jax.ShapeDtypeStruct((8 * slots + LIST_TAIL, LANES), jnp.bfloat16),
        in_specs=[SMEM, SMEM, VMEM, VMEM, VMEM, VMEM, VMEM],
        out_specs=VMEM,
        scratch_shapes=[
            pltpu.VMEM((2 * first.shape[0] + 3 * 8 * SHARE, LANES), jnp.float32),
            pltpu.VMEM((8 * slots, LANES), jnp.float32),
        ],
        compiler_params=PARAMS,
        cost_estimate=LITTLE,
    )(places, counts, first, second, own, tiles, tail)


def forward_kernel(places_ref, goals_ref, counts_ref, here_ref, there_ref, tiles_ref, first_ref, second_ref, own_ref, wide, sums):
    slots = tiles_ref.shape[0]
    half = here_ref.shape[0]
    part = first_ref.shape[0]
    wide[:half, :] = here_ref[...].astype(jnp.float32)
    wide[half:, :] = there_ref[...].astype(jnp.float32)
    sums[...] = jnp.zeros_like(sums)
    lanes = lax.broadcasted_iota(jnp.int32, (8, LANES), 1)
    for slot in range(slots):
        x = wide[pl.ds(pl.multiple_of(places_ref[slot] * 8, 8), 8), :].astype(jnp.bfloat16)
        y = lax.dot_general(x, tiles_ref[slot], (((1,), (1,)), ((), ())), preferred_element_type=jnp.float32)
        y = jnp.where(lanes < counts_ref[slot], y, 0.0)
        sums[pl.ds(goals_ref[slot], 8, stride=SHARE), :] = y
    first_ref[...] = sums[:part, :].astype(jnp.bfloat16)
    second_ref[...] = sums[part : 2 * part, :].astype(jnp.bfloat16)
    own_ref[...] = sums[2 * part : -8 * SHARE, :].astype(jnp.bfloat16)


def forward_products(places, goals, counts, here, there, tiles, cols):
    part = cols * 8 * SHARE
    shape = jax.ShapeDtypeStruct((part, LANES), jnp.bfloat16)
    own = jax.ShapeDtypeStruct((2 * 8 * SHARE, LANES), jnp.bfloat16)
    return pl.pallas_call(
        forward_kernel,
        out_shape=(shape, shape, own),
        in_specs=[SMEM, SMEM, SMEM, VMEM, VMEM, VMEM],
        out_specs=(VMEM, VMEM, VMEM),
        scratch_shapes=[
            pltpu.VMEM((2 * here.shape[0], LANES), jnp.float32),
            pltpu.VMEM((2 * part + 3 * 8 * SHARE, LANES), jnp.float32),
        ],
        compiler_params=PARAMS,
        cost_estimate=LITTLE,
    )(places, goals, counts, here, there, tiles)


def sum_kernel(cols, slots, place_ref, most_ref, asked_ref, first_ref, second_ref, own_ref, *refs):
    lists, (out_ref, acc) = refs[:-2], refs[-2:]
    tiles_here = out_ref.shape[0] // 8
    rows = 8 * slots + LIST_TAIL
    near = lax.broadcasted_iota(jnp.int32, (tiles_here, LANES), 0)
    own = (near + place_ref[2]).astype(jnp.float32)
    acc[...] = jnp.zeros_like(acc)

    def add_forward(ref, askers):
        chosen = [chosen_of(asked_ref, col, near)[:, start : start + SHARE] for col, start in askers]
        chosen = jnp.concatenate(chosen, axis=1).astype(jnp.bfloat16)
        for vec in range(8):
            values = [ref[(i * 8 + vec) * SHARE : (i * 8 + vec + 1) * SHARE, :] for i in range(len(askers))]
            acc[vec] += jnp.dot(chosen, jnp.concatenate(values, axis=0), preferred_element_type=jnp.float32)

    add_forward(first_ref, [(col, 0) for col in range(cols)])
    add_forward(own_ref, [(place_ref[0], 0), (place_ref[0], SHARE)])

    @pl.when(most_ref[0] > SHARE)
    def _():
        add_forward(second_ref, [(col, SHARE) for col in range(cols)])

    for part in lists:
        for start in range(0, part.shape[0], rows):
            digits = part[start + 8 * slots : start + rows, :].astype(jnp.float32)
            ids = digits[0:1] + 64.0 * digits[1:2] + 4096.0 * digits[2:3]
            chosen = jnp.where(own == ids, 1.0, 0.0)[:, :slots].astype(jnp.bfloat16)
            for vec in range(8):
                values = part[start + vec * slots : start + (vec + 1) * slots, :]
                acc[vec] += jnp.dot(chosen, values, preferred_element_type=jnp.float32)
    for vec in range(8):
        out_ref[pl.ds(vec, tiles_here, stride=8), :] = acc[vec]


def summed(place, most, asked, first, second, own, lists, slots, cols, tiles_here):
    return pl.pallas_call(
        functools.partial(sum_kernel, cols, slots),
        out_shape=jax.ShapeDtypeStruct((8 * tiles_here, LANES), jnp.float32),
        in_specs=[SMEM, SMEM] + [VMEM] * (4 + len(lists)),
        out_specs=VMEM,
        scratch_shapes=[pltpu.VMEM((8, tiles_here, LANES), jnp.float32)],
        compiler_params=PARAMS,
    )(place, most, asked, first, second, own, *lists)


def tail_of(ids):
    digits = jnp.stack([jnp.where(ids < 0, ids, ids % 64), jnp.maximum(ids, 0) // 64 % 64, jnp.maximum(ids, 0) // 4096])
    return jnp.pad(digits.astype(jnp.bfloat16), ((0, LIST_TAIL - 3), (0, LANES - ids.shape[0])))


def local(vectors, tiles, tile_rows, tile_cols, row_counts, live_tiles):
    vec_count, seg_len = vectors.shape
    slots, tile_len = tiles.shape[:2]
    rows, cols = lax.axis_size("row"), lax.axis_size("col")
    per_piece = seg_len // tile_len
    row, col = lax.axis_index("row"), lax.axis_index("col")
    grid = (rows, cols)
    join = functools.partial(jnp.concatenate, axis=0)

    live = jnp.arange(slots, dtype=jnp.int32) < live_tiles[0]
    counts = jnp.where(live, row_counts, 0)
    col_row = tile_cols // (cols * per_piece)
    group = col_row // 4 - row // 4
    other = (col_row % 4) ^ (row % 4)
    col_part = (other & 1) * 5 + jnp.where(group == 2, 4, (other >> 1) + 2 * group)
    col_places = col_part * per_piece + tile_cols % per_piece
    tail = tail_of(jnp.where(live, tile_cols, -1))

    rounded = vectors.astype(jnp.bfloat16).reshape(vec_count, per_piece, tile_len).transpose(1, 0, 2).reshape(-1, tile_len)
    place = jnp.stack([col, row * cols * per_piece, (row * cols + col) * per_piece])
    wanted, row_places = requests(place, tile_rows, live_tiles, cols, per_piece)
    across = across_halves(rounded, *grid)
    asked = lax.all_to_all(wanted, "col", 0, 0)
    most = jnp.max(asked[:, 1, 0])
    reply, late_reply, own_reply = replies(place, asked, rounded, cols, slots)
    both = join([rounded, after(across, reply)])
    groups = next_groups(both, *grid, -1)
    reply = over_columns(reply, cols)
    late_reply = lax.cond(most > SHARE, lambda v: over_columns(v, cols), lambda v: v, late_reply)
    here = join([both, *groups])
    there = other_core(here, *grid)
    mirror = mirror_products(row_places, counts, after(reply, here), late_reply, own_reply, tiles, tail)
    mirror_across = across_halves(mirror, *grid)
    there = after(there, mirror)
    forward, late_forward, own_forward = forward_products(col_places, row_places, counts, here, there, tiles, cols)
    mirror_both = join([mirror, after(mirror_across, forward)])
    mirror_groups = next_groups(mirror_both, *grid, 1)
    forward = over_columns(after(forward, mirror_both), cols)
    late_forward = lax.cond(most > SHARE, lambda v: over_columns(v, cols), lambda v: v, late_forward)
    mirror_here = after(join([mirror_both, *mirror_groups]), late_forward)
    mirror_there = other_core(mirror_here, *grid)
    lists = [mirror_here, mirror_there]
    total = summed(place, most.reshape(1), asked, forward, late_forward, own_forward, lists, slots, cols, per_piece)
    return total.reshape(per_piece, vec_count, tile_len).transpose(1, 0, 2).reshape(vec_count, seg_len)


def solution(mesh):
    placed = (
        P(None, AXES),
        P(AXES, None, None),
        P(AXES),
        P(AXES),
        P(AXES),
        P(AXES),
    )
    return jax.shard_map(local, mesh=mesh, in_specs=placed, out_specs=P(None, AXES), check_vma=False)
```

time: 138 us -> 116 us (0.84)
  the two profiles are of different devices: /device:TPU:7 before, /device:TPU:26 now
where the time goes in v2:
time: 116 us
  starting transfers between devices  44.8 us (39%)
  waiting for transfers between devices  35.3 us (30%)
  blocking collectives  15.1 us (13%)
  Pallas kernels  12.9 us (11%)
  other arithmetic  5.41 us (5%)
  between operations  1.48 us (1%)
    ppermute x8, starting transfers between devices, send(): return lax.ppermute(value, AXES, moves)  35.7 us
    all_to_all x2, waiting for transfers between devices, over_columns(): lax.all_to_all(value.reshape(cols, -1, LANES), 'col', 0, 0)  19.9 us
    ppermute x8, waiting for transfers between devices, send(): return lax.ppermute(value, AXES, moves)  15.4 us
    all_to_all x1, blocking collectives, local(): asked = lax.all_to_all(wanted, 'col', 0, 0)  15.1 us
    all_to_all x2, starting transfers between devices, over_columns(): lax.all_to_all(value.reshape(cols, -1, LANES), 'col', 0, 0)  9.16 us
    pallas_call x1, Pallas kernels, forward_products(): pl.pallas_call(forward_kernel, out_shape=(shape, shape, own), in_specs=[S...  3.74 us
    pallas_call x1, Pallas kernels, summed(): pl.pallas_call(functools.partial(sum_kernel, cols, slots), out_shape=jax....  3.01 us
  transfers between devices with their start and end apart: 10, of which 6 were waited for; matrix products, arithmetic and copies ran while one was open for 3% of the time, Pallas kernels for 9%

profile of v2, /device:TPU:26, one launch (start us, length us, event | category | flops | bytes accessed | tf_op | source)
XLA Modules:
  0.0 115.6 jit_solution(374744326902570251)
XLA Ops:
  0.0 1.0 convert_bitcast_fusion.x_ref
  1.0 15.1 %collective-permute-start = (bf16[768,128]{1,0:T(8,128)(2,1)S(1)}, bf16[768,128]{1,0:T(8,128)(2,1)S(1)}, u32[]{:S(2)}, u32[]{:S(2)}) collective-permute-start(bf16[768,128]{1,0:T(8,128)(2,1)S(1)} %convert_bitcast_fusion.x_ref), channel_id=1, source_target_pairs={{0,12},{1,13},{2,14},{3,15},{4,16},{5,17},{6,18},{7,19},{8,20},{9,... | collective-permute-start | bytes 589832 | tf_op jit(solution)/shard_map/ppermute | solution.py:22
  17.4 2.3 %shard_map.64 = (s32[6,8,128]{2,1,0:T(8,128)}, s32[64]{0:T(128)}) custom-call(s32[3]{0:T(128)} %pad_add_fusion.place_ref, s32[64]{0:T(128)} %rows_ref.1, s32[1]{0:T(128)} %copy.11.live_ref), custom_call_target="tpu_custom_call" | custom-call | tf_op jit(solution)/shard_map/pallas_call | solution.py:91
  19.7 15.1 %all_to_all.25.asked_ref = s32[6,8,128]{2,1,0:T(8,128)S(1)} all-to-all(s32[6,8,128]{2,1,0:T(8,128)} %get-tuple-element.29), channel_id=1, replica_groups=mesh['row'=128,'col'=6] {'col'}, dimensions={0} | all-to-all | bytes 49152 | tf_op jit(solution)/shard_map/all_to_all | solution.py:286
  35.4 1.9 %shard_map.65 = (bf16[1536,128]{1,0:T(8,128)(2,1)}, bf16[1536,128]{1,0:T(8,128)(2,1)S(1)}, bf16[512,128]{1,0:T(8,128)(2,1)S(1)}) custom-call(s32[3]{0:T(128)S(1)} %copy-done.1, s32[6,8,128]{2,1,0:T(8,128)S(1)} %all_to_all.25.asked_ref, bf16[768,128]{1,0:T(8,128)(2,1)S(1)} %convert_bitcast_fusion.x_ref), custom_call_target="tpu_custom_call" | custom-call | tf_op jit(solution)/shard_map/pallas_call | solution.py:134
  37.3 2.4 %collective-permute-start.1 = (bf16[1536,128]{1,0:T(8,128)(2,1)S(1)}, bf16[1536,128]{1,0:T(8,128)(2,1)}, u32[]{:S(2)}, u32[]{:S(2)}) collective-permute-start(bf16[1536,128]{1,0:T(8,128)(2,1)S(1)} %pad_maximum_fusion.2), channel_id=1, source_target_pairs={{24,0},{25,1},{26,2},{27,3},{28,4},{29,5},{30,6},{31,7},{32,8},{33... | collective-permute-start | bytes 1179656 | tf_op jit(solution)/shard_map/ppermute | solution.py:22
  39.7 1.3 %collective-permute-start.2 = (bf16[768,128]{1,0:T(8,128)(2,1)S(1)}, bf16[768,128]{1,0:T(8,128)(2,1)}, u32[]{:S(2)}, u32[]{:S(2)}) collective-permute-start(bf16[768,128]{1,0:T(8,128)(2,1)S(1)} %collective-permute-done), channel_id=1, source_target_pairs={{60,12},{61,13},{62,14},{63,15},{64,16},{65,17},{66,18},{67,19},{6... | collective-permute-start | bytes 589832 | tf_op jit(solution)/shard_map/ppermute | solution.py:22
  42.3 4.3 %all-to-all-start.3 = ((bf16[6,256,128]{2,1,0:T(8,128)(2,1)}), bf16[6,256,128]{2,1,0:T(8,128)(2,1)}, u32[]{:S(2)}, u32[]{:S(2)}) async-start(bf16[6,256,128]{2,1,0:T(8,128)(2,1)} %bitcast.14), calls=%async_computation.3 | async-start | bytes 786432 | tf_op jit(solution)/shard_map/all_to_all | solution.py:56
  46.6 3.1 %collective-permute-done.1 = bf16[1536,128]{1,0:T(8,128)(2,1)} collective-permute-done((bf16[1536,128]{1,0:T(8,128)(2,1)S(1)}, bf16[1536,128]{1,0:T(8,128)(2,1)}, u32[]{:S(2)}, u32[]{:S(2)}) %collective-permute-start.1) | collective-permute-done | bytes 393248 | tf_op jit(solution)/shard_map/ppermute | solution.py:22
  49.7 1.2 %pad_maximum_fusion.here_ref = bf16[3840,128]{1,0:T(8,128)(2,1)S(1)} fusion(bf16[768,128]{1,0:T(8,128)(2,1)} %collective-permute-done.2, bf16[1536,128]{1,0:T(8,128)(2,1)} %collective-permute-done.1, bf16[768,128]{1,0:T(8,128)(2,1)} %copy-done.6, bf16[768,128]{1,0:T(8,128)(2,1)S(1)} %convert_bitcast_fusion.x_ref), kind=kLoop, calls=%fused_computation | loop fusion | flops 3932160 | bytes 1966080 | tf_op jit(solution)/shard_map/concatenate | solution.py:293
  50.9 1.9 %collective-permute-start.3 = (bf16[3840,128]{1,0:T(8,128)(2,1)S(1)}, bf16[3840,128]{1,0:T(8,128)(2,1)}, u32[]{:S(2)}, u32[]{:S(2)}) collective-permute-start(bf16[3840,128]{1,0:T(8,128)(2,1)S(1)} %pad_maximum_fusion.here_ref), channel_id=1, source_target_pairs={{0,6},{1,7},{2,8},{3,9},{4,10},{5,11},{6,0},{7,1},{8,2},{9,3},{10,... | collective-permute-start | bytes 2949128 | tf_op jit(solution)/shard_map/ppermute | solution.py:22
  52.9 9.8 %all-to-all-done.3 = bf16[6,256,128]{2,1,0:T(8,128)(2,1)} async-done(((bf16[6,256,128]{2,1,0:T(8,128)(2,1)}), bf16[6,256,128]{2,1,0:T(8,128)(2,1)}, u32[]{:S(2)}, u32[]{:S(2)}) %all-to-all-start.3) | async-done | bytes 393248 | tf_op jit(solution)/shard_map/all_to_all | solution.py:56
  62.7 1.9 %shard_map.66 = bf16[528,128]{1,0:T(8,128)(2,1)S(1)} custom-call(s32[64]{0:T(128)S(1)} %copy-done.3, s32[64]{0:T(128)S(1)} %get-tuple-element.47.counts_ref, bf16[1536,128]{1,0:T(8,128)(2,1)} %bitcast.15.first_ref, bf16[1536,128]{1,0:T(8,128)(2,1)} %copy-done.5, bf16[512,128]{1,0:T(8,128)(2,1)S(1)} %get-tuple-element.35.own_ref, ...), custom_call_target="tpu_custom_call" | custom-call | tf_op jit(solution)/shard_map/pallas_call | solution.py:164
  64.6 6.4 %collective-permute-start.4 = (bf16[528,128]{1,0:T(8,128)(2,1)S(1)}, bf16[528,128]{1,0:T(8,128)(2,1)}, u32[]{:S(2)}, u32[]{:S(2)}) collective-permute-start(bf16[528,128]{1,0:T(8,128)(2,1)S(1)} %shard_map.66), channel_id=1, source_target_pairs={{0,12},{1,13},{2,14},{3,15},{4,16},{5,17},{6,18},{7,19},{8,20},{9,... | collective-permute-start | bytes 405512 | tf_op jit(solution)/shard_map/ppermute | solution.py:22
  71.0 3.7 %shard_map.67 = (bf16[1536,128]{1,0:T(8,128)(2,1)}, bf16[1536,128]{1,0:T(8,128)(2,1)}, bf16[512,128]{1,0:T(8,128)(2,1)S(1)}) custom-call(s32[64]{0:T(128)S(1)} %get-tuple-element.46.places_ref, s32[64]{0:T(128)S(1)} %copy-done.3, s32[64]{0:T(128)S(1)} %get-tuple-element.47.counts_ref, bf16[3840,128]{1,0:T(8,128)(2,1)S(1)} %pad_maximum_fusion.here_ref, ...), custom_call_target="tpu_custom_call" | custom-call | tf_op jit(solution)/shard_map/pallas_call | solution.py:200
  74.8 8.2 %collective-permute-done.4 = bf16[528,128]{1,0:T(8,128)(2,1)} collective-permute-done((bf16[528,128]{1,0:T(8,128)(2,1)S(1)}, bf16[528,128]{1,0:T(8,128)(2,1)}, u32[]{:S(2)}, u32[]{:S(2)}) %collective-permute-start.4) | collective-permute-done | bytes 135200 | tf_op jit(solution)/shard_map/ppermute | solution.py:22
  83.9 4.7 %collective-permute-start.5 = (bf16[1056,128]{1,0:T(8,128)(2,1)S(1)}, bf16[1056,128]{1,0:T(8,128)(2,1)S(1)}, u32[]{:S(2)}, u32[]{:S(2)}) collective-permute-start(bf16[1056,128]{1,0:T(8,128)(2,1)S(1)} %pad_maximum_fusion.3), channel_id=1, source_target_pairs={{0,24},{1,25},{2,26},{3,27},{4,28},{5,29},{6,30},{7,31},{8,32},{9,... | collective-permute-start | bytes 811016 | tf_op jit(solution)/shard_map/ppermute | solution.py:22
  88.6 1.9 %collective-permute-start.6 = (bf16[528,128]{1,0:T(8,128)(2,1)}, bf16[528,128]{1,0:T(8,128)(2,1)S(1)}, u32[]{:S(2)}, u32[]{:S(2)}) collective-permute-start(bf16[528,128]{1,0:T(8,128)(2,1)} %collective-permute-done.4), channel_id=1, source_target_pairs={{0,48},{1,49},{2,50},{3,51},{4,52},{5,53},{6,54},{7,55},{8,56},{9,... | collective-permute-start | bytes 405512 | tf_op jit(solution)/shard_map/ppermute | solution.py:22
  90.6 4.9 %all-to-all-start.4 = ((bf16[6,256,128]{2,1,0:T(8,128)(2,1)}), bf16[6,256,128]{2,1,0:T(8,128)(2,1)S(1)}, u32[]{:S(2)}, u32[]{:S(2)}) async-start(bf16[6,256,128]{2,1,0:T(8,128)(2,1)} %bitcast.19), calls=%async_computation.4 | async-start | bytes 786432 | tf_op jit(solution)/shard_map/all_to_all | solution.py:56
  95.5 1.9 %collective-permute-done.6 = bf16[528,128]{1,0:T(8,128)(2,1)S(1)} collective-permute-done((bf16[528,128]{1,0:T(8,128)(2,1)}, bf16[528,128]{1,0:T(8,128)(2,1)S(1)}, u32[]{:S(2)}, u32[]{:S(2)}) %collective-permute-start.6) | collective-permute-done | bytes 135200 | tf_op jit(solution)/shard_map/ppermute | solution.py:22
  98.4 1.9 %collective-permute-start.7 = (bf16[2640,128]{1,0:T(8,128)(2,1)S(1)}, bf16[2640,128]{1,0:T(8,128)(2,1)S(1)}, u32[]{:S(2)}, u32[]{:S(2)}) collective-permute-start(bf16[2640,128]{1,0:T(8,128)(2,1)S(1)} %pad_maximum_fusion.1.refs_0_), channel_id=1, source_target_pairs={{0,6},{1,7},{2,8},{3,9},{4,10},{5,11},{6,0},{7,1},{8,2},{9,3},{10,... | collective-permute-start | bytes 2027528 | tf_op jit(solution)/shard_map/ppermute | solution.py:22
  100.3 2.1 %collective-permute-done.7.refs_1_ = bf16[2640,128]{1,0:T(8,128)(2,1)S(1)} collective-permute-done((bf16[2640,128]{1,0:T(8,128)(2,1)S(1)}, bf16[2640,128]{1,0:T(8,128)(2,1)S(1)}, u32[]{:S(2)}, u32[]{:S(2)}) %collective-permute-start.7) | collective-permute-done | bytes 675872 | tf_op jit(solution)/shard_map/ppermute | solution.py:22
  102.4 10.1 %all-to-all-done.4 = bf16[6,256,128]{2,1,0:T(8,128)(2,1)S(1)} async-done(((bf16[6,256,128]{2,1,0:T(8,128)(2,1)}), bf16[6,256,128]{2,1,0:T(8,128)(2,1)S(1)}, u32[]{:S(2)}, u32[]{:S(2)}) %all-to-all-start.4) | async-done | bytes 393248 | tf_op jit(solution)/shard_map/all_to_all | solution.py:56
  112.6 3.0 %shard_map.68 = f32[768,128]{1,0:T(8,128)} custom-call(s32[3]{0:T(128)S(1)} %copy-done.2, s32[1]{0:T(128)} %bitcast.7.most_ref, s32[6,8,128]{2,1,0:T(8,128)S(1)} %all_to_all.25.asked_ref, bf16[1536,128]{1,0:T(8,128)(2,1)S(1)} %bitcast.31, bf16[1536,128]{1,0:T(8,128)(2,1)S(1)} %copy-done.4, bf16[512,128]{1,0:T(8,128)(2,1)S(1)} %get-tuple-element.41.own_ref, ...), custom_call_target="tpu_custom_call" | custom-call | tf_op jit(solution)/shard_map/pallas_call | solution.py:249
  (31 shorter events, 3.9 us)
Async XLA Ops:
  1.0 36.3 %collective-permute-start = (bf16[768,128]{1,0:T(8,128)(2,1)S(1)}, bf16[768,128]{1,0:T(8,128)(2,1)S(1)}, u32[]{:S(2)}, u32[]{:S(2)}) collective-permute-start(bf16[768,128]{1,0:T(8,128)(2,1)S(1)} %convert_bitcast_fusion.x_ref), channel_id=1, source_target_pairs={{0,12},{1,13},{2,14},{3,15},{4,16},{5,17},{6,18},{7,19},{8,20},{9,... | collective-permute-start | bytes 589832 | tf_op jit(solution)/shard_map/ppermute | solution.py:22
  34.8 0.6 copy-start.1
  37.3 9.3 %copy-start.6 = (bf16[768,128]{1,0:T(8,128)(2,1)}, bf16[768,128]{1,0:T(8,128)(2,1)S(1)}, u32[]{:S(2)}) copy-start(bf16[768,128]{1,0:T(8,128)(2,1)S(1)} %collective-permute-done) | copy-start | bytes 589828
  37.3 12.4 %collective-permute-start.1 = (bf16[1536,128]{1,0:T(8,128)(2,1)S(1)}, bf16[1536,128]{1,0:T(8,128)(2,1)}, u32[]{:S(2)}, u32[]{:S(2)}) collective-permute-start(bf16[1536,128]{1,0:T(8,128)(2,1)S(1)} %pad_maximum_fusion.2), channel_id=1, source_target_pairs={{24,0},{25,1},{26,2},{27,3},{28,4},{29,5},{30,6},{31,7},{32,8},{33... | collective-permute-start | bytes 1179656 | tf_op jit(solution)/shard_map/ppermute | solution.py:22
  39.7 6.9 %collective-permute-start.2 = (bf16[768,128]{1,0:T(8,128)(2,1)S(1)}, bf16[768,128]{1,0:T(8,128)(2,1)}, u32[]{:S(2)}, u32[]{:S(2)}) collective-permute-start(bf16[768,128]{1,0:T(8,128)(2,1)S(1)} %collective-permute-done), channel_id=1, source_target_pairs={{60,12},{61,13},{62,14},{63,15},{64,16},{65,17},{66,18},{67,19},{6... | collective-permute-start | bytes 589832 | tf_op jit(solution)/shard_map/ppermute | solution.py:22
  42.2 10.6 %copy-start.7 = (s32[64]{0:T(128)S(1)}, s32[64]{0:T(128)}, u32[]{:S(2)}) copy-start(s32[64]{0:T(128)} %param.13) | copy-start | bytes 772
  42.2 10.6 %copy-start.8 = (s32[64]{0:T(128)S(1)}, s32[64]{0:T(128)}, u32[]{:S(2)}) copy-start(s32[64]{0:T(128)} %param.14) | copy-start | bytes 772
  42.3 20.4 %copy-start = (bf16[64,128,128]{2,1,0:T(8,128)(2,1)S(1)}, bf16[64,128,128]{2,1,0:T(8,128)(2,1)}, u32[]{:S(2)}) copy-start(bf16[64,128,128]{2,1,0:T(8,128)(2,1)} %tiles_ref.3) | copy-start | bytes 6291460
  42.3 20.4 %copy-start.3 = (s32[64]{0:T(128)S(1)}, s32[64]{0:T(128)}, u32[]{:S(2)}) copy-start(s32[64]{0:T(128)} %get-tuple-element.30.places_ref.goals_ref) | copy-start | bytes 772
  42.3 4.3 %copy-start.5 = (bf16[1536,128]{1,0:T(8,128)(2,1)}, bf16[1536,128]{1,0:T(8,128)(2,1)S(1)}, u32[]{:S(2)}) copy-start(bf16[1536,128]{1,0:T(8,128)(2,1)S(1)} %get-tuple-element.48.second_ref) | copy-start | bytes 1179652
  42.3 20.4 %all-to-all-start.3 = ((bf16[6,256,128]{2,1,0:T(8,128)(2,1)}), bf16[6,256,128]{2,1,0:T(8,128)(2,1)}, u32[]{:S(2)}, u32[]{:S(2)}) async-start(bf16[6,256,128]{2,1,0:T(8,128)(2,1)} %bitcast.14), calls=%async_computation.3 | async-start | bytes 786432 | tf_op jit(solution)/shard_map/all_to_all | solution.py:56
  50.9 20.1 %collective-permute-start.3 = (bf16[3840,128]{1,0:T(8,128)(2,1)S(1)}, bf16[3840,128]{1,0:T(8,128)(2,1)}, u32[]{:S(2)}, u32[]{:S(2)}) collective-permute-start(bf16[3840,128]{1,0:T(8,128)(2,1)S(1)} %pad_maximum_fusion.here_ref), channel_id=1, source_target_pairs={{0,6},{1,7},{2,8},{3,9},{4,10},{5,11},{6,0},{7,1},{8,2},{9,3},{10,... | collective-permute-start | bytes 2949128 | tf_op jit(solution)/shard_map/ppermute | solution.py:22
  64.6 18.3 %collective-permute-start.4 = (bf16[528,128]{1,0:T(8,128)(2,1)S(1)}, bf16[528,128]{1,0:T(8,128)(2,1)}, u32[]{:S(2)}, u32[]{:S(2)}) collective-permute-start(bf16[528,128]{1,0:T(8,128)(2,1)S(1)} %shard_map.66), channel_id=1, source_target_pairs={{0,12},{1,13},{2,14},{3,15},{4,16},{5,17},{6,18},{7,19},{8,20},{9,... | collective-permute-start | bytes 405512 | tf_op jit(solution)/shard_map/ppermute | solution.py:22
  83.9 28.6 %copy-start.2 = (s32[3]{0:T(128)S(1)}, s32[3]{0:T(128)}, u32[]{:S(2)}) copy-start(s32[3]{0:T(128)} %pad_add_fusion.place_ref) | copy-start | bytes 40
  83.9 13.5 %collective-permute-start.5 = (bf16[1056,128]{1,0:T(8,128)(2,1)S(1)}, bf16[1056,128]{1,0:T(8,128)(2,1)S(1)}, u32[]{:S(2)}, u32[]{:S(2)}) collective-permute-start(bf16[1056,128]{1,0:T(8,128)(2,1)S(1)} %pad_maximum_fusion.3), channel_id=1, source_target_pairs={{0,24},{1,25},{2,26},{3,27},{4,28},{5,29},{6,30},{7,31},{8,32},{9,... | collective-permute-start | bytes 811016 | tf_op jit(solution)/shard_map/ppermute | solution.py:22
  88.6 8.8 %collective-permute-start.6 = (bf16[528,128]{1,0:T(8,128)(2,1)}, bf16[528,128]{1,0:T(8,128)(2,1)S(1)}, u32[]{:S(2)}, u32[]{:S(2)}) collective-permute-start(bf16[528,128]{1,0:T(8,128)(2,1)} %collective-permute-done.4), channel_id=1, source_target_pairs={{0,48},{1,49},{2,50},{3,51},{4,52},{5,53},{6,54},{7,55},{8,56},{9,... | collective-permute-start | bytes 405512 | tf_op jit(solution)/shard_map/ppermute | solution.py:22
  90.6 22.0 %copy-start.4 = (bf16[1536,128]{1,0:T(8,128)(2,1)S(1)}, bf16[1536,128]{1,0:T(8,128)(2,1)}, u32[]{:S(2)}) copy-start(bf16[1536,128]{1,0:T(8,128)(2,1)} %get-tuple-element.49.second_ref) | copy-start | bytes 1179652
  90.6 22.0 %all-to-all-start.4 = ((bf16[6,256,128]{2,1,0:T(8,128)(2,1)}), bf16[6,256,128]{2,1,0:T(8,128)(2,1)S(1)}, u32[]{:S(2)}, u32[]{:S(2)}) async-start(bf16[6,256,128]{2,1,0:T(8,128)(2,1)} %bitcast.19), calls=%async_computation.4 | async-start | bytes 786432 | tf_op jit(solution)/shard_map/all_to_all | solution.py:56
  98.4 4.0 %collective-permute-start.7 = (bf16[2640,128]{1,0:T(8,128)(2,1)S(1)}, bf16[2640,128]{1,0:T(8,128)(2,1)S(1)}, u32[]{:S(2)}, u32[]{:S(2)}) collective-permute-start(bf16[2640,128]{1,0:T(8,128)(2,1)S(1)} %pad_maximum_fusion.1.refs_0_), channel_id=1, source_target_pairs={{0,6},{1,7},{2,8},{3,9},{4,10},{5,11},{6,0},{7,1},{8,2},{9,3},{10,... | collective-permute-start | bytes 2027528 | tf_op jit(solution)/shard_map/ppermute | solution.py:22

commit v3 on v2

--- a/solution.py
+++ b/solution.py
@@ -60,7 +60,7 @@
     return lax.optimization_barrier((value, *others))[0]
 
 
-def request_kernel(cols, per_piece, place_ref, rows_ref, live_ref, ids_ref, places_ref, used):
+def request_kernel(cols, per_piece, place_ref, rows_ref, live_ref, ids_ref, places_ref, used, seen):
     slots = rows_ref.shape[0]
     me, start = place_ref[0], place_ref[1]
     for col in range(cols):
@@ -72,9 +72,14 @@
         for edge in range(1, cols):
             col = col + jnp.where(tile >= edge * per_piece, 1, 0)
         here = slot < live
-        rank = used[col]
-        used[col] = rank + jnp.where(here, 1, 0)
-        ids_ref[col, 0, rank] = tile - col * per_piece
+        near = tile - col * per_piece
+        count = used[col]
+        known = jnp.minimum(seen[tile], slots - 1)
+        again = (seen[tile] >= 0) & (seen[tile] < count) & (ids_ref[col, 0, jnp.maximum(known, 0)] == near)
+        rank = jnp.where(again, known, count)
+        used[col] = count + jnp.where(here & jnp.logical_not(again), 1, 0)
+        ids_ref[col, 0, rank] = near
+        seen[tile] = rank
         late = jnp.where(rank < SHARE, 0, 1)
         chunk = jnp.where(col == me, 2 * cols + late, col + cols * late)
         places_ref[slot] = jnp.where(here, chunk * (8 * SHARE) + rank - late * SHARE, (2 * cols + 2) * 8 * SHARE)
@@ -96,7 +101,7 @@
         ),
         in_specs=[SMEM, SMEM, SMEM],
         out_specs=(SMEM, SMEM),
-        scratch_shapes=[pltpu.SMEM((cols,), jnp.int32)],
+        scratch_shapes=[pltpu.SMEM((cols,), jnp.int32), pltpu.SMEM((cols * per_piece,), jnp.int32)],
         cost_estimate=LITTLE,
     )(place, tile_rows, live_tiles)
 
@@ -187,7 +192,7 @@
         x = wide[pl.ds(pl.multiple_of(places_ref[slot] * 8, 8), 8), :].astype(jnp.bfloat16)
         y = lax.dot_general(x, tiles_ref[slot], (((1,), (1,)), ((), ())), preferred_element_type=jnp.float32)
         y = jnp.where(lanes < counts_ref[slot], y, 0.0)
-        sums[pl.ds(goals_ref[slot], 8, stride=SHARE), :] = y
+        sums[pl.ds(goals_ref[slot], 8, stride=SHARE), :] += y
     first_ref[...] = sums[:part, :].astype(jnp.bfloat16)
     second_ref[...] = sums[part : 2 * part, :].astype(jnp.bfloat16)
     own_ref[...] = sums[2 * part : -8 * SHARE, :].astype(jnp.bfloat16)

time: 116 us -> 117 us (level)
  the two profiles are of different devices: /device:TPU:26 before, /device:TPU:7 now
where the time goes in v3:
time: 117 us; the launch traced here: 115 us
  starting transfers between devices  61.1 us (52%)
  waiting for transfers between devices  19.4 us (17%)
  blocking collectives  13.6 us (12%)
  Pallas kernels  13.3 us (11%)
  other arithmetic  5.41 us (5%)
  between operations  1.49 us (1%)
    ppermute x8, starting transfers between devices, send(): return lax.ppermute(value, AXES, moves)  47.8 us
    all_to_all x2, waiting for transfers between devices, over_columns(): lax.all_to_all(value.reshape(cols, -1, LANES), 'col', 0, 0)  17.2 us
    all_to_all x1, blocking collectives, local(): asked = lax.all_to_all(wanted, 'col', 0, 0)  13.6 us
    all_to_all x2, starting transfers between devices, over_columns(): lax.all_to_all(value.reshape(cols, -1, LANES), 'col', 0, 0)  13.3 us
    pallas_call x1, Pallas kernels, forward_products(): pl.pallas_call(forward_kernel, out_shape=(shape, shape, own), in_specs=[S...  3.73 us
    pallas_call x1, Pallas kernels, summed(): pl.pallas_call(functools.partial(sum_kernel, cols, slots), out_shape=jax....  3 us
    pallas_call x1, Pallas kernels, requests(): pl.pallas_call(functools.partial(request_kernel, cols, per_piece), out_sh...  2.8 us
  transfers between devices with their start and end apart: 10, of which 4 were waited for; matrix products, arithmetic and copies ran while one was open for 3% of the time, Pallas kernels for 9%

profile of v3, /device:TPU:7, one launch (start us, length us, event | category | flops | bytes accessed | tf_op | source)
XLA Modules:
  0.0 115.1 jit_solution(7220132892355136393)
XLA Ops:
  0.0 1.0 convert_bitcast_fusion.x_ref
  1.0 14.9 %collective-permute-start = (bf16[768,128]{1,0:T(8,128)(2,1)S(1)}, bf16[768,128]{1,0:T(8,128)(2,1)S(1)}, u32[]{:S(2)}, u32[]{:S(2)}) collective-permute-start(bf16[768,128]{1,0:T(8,128)(2,1)S(1)} %convert_bitcast_fusion.x_ref), channel_id=1, source_target_pairs={{0,12},{1,13},{2,14},{3,15},{4,16},{5,17},{6,18},{7,19},{8,20},{9,... | collective-permute-start | bytes 589832 | tf_op jit(solution)/shard_map/ppermute | solution.py:22
  17.1 2.8 %shard_map.64 = (s32[6,8,128]{2,1,0:T(8,128)}, s32[64]{0:T(128)}) custom-call(s32[3]{0:T(128)} %pad_add_fusion.place_ref, s32[64]{0:T(128)} %rows_ref.1, s32[1]{0:T(128)} %copy.11.live_ref), custom_call_target="tpu_custom_call" | custom-call | tf_op jit(solution)/shard_map/pallas_call | solution.py:96
  20.0 13.6 %all_to_all.25.asked_ref = s32[6,8,128]{2,1,0:T(8,128)S(1)} all-to-all(s32[6,8,128]{2,1,0:T(8,128)} %get-tuple-element.29), channel_id=1, replica_groups=mesh['row'=128,'col'=6] {'col'}, dimensions={0} | all-to-all | bytes 49152 | tf_op jit(solution)/shard_map/all_to_all | solution.py:291
  34.2 1.9 %shard_map.65 = (bf16[1536,128]{1,0:T(8,128)(2,1)}, bf16[1536,128]{1,0:T(8,128)(2,1)S(1)}, bf16[512,128]{1,0:T(8,128)(2,1)S(1)}) custom-call(s32[3]{0:T(128)S(1)} %copy-done.1, s32[6,8,128]{2,1,0:T(8,128)S(1)} %all_to_all.25.asked_ref, bf16[768,128]{1,0:T(8,128)(2,1)S(1)} %convert_bitcast_fusion.x_ref), custom_call_target="tpu_custom_call" | custom-call | tf_op jit(solution)/shard_map/pallas_call | solution.py:139
  36.1 5.4 %collective-permute-start.1 = (bf16[1536,128]{1,0:T(8,128)(2,1)S(1)}, bf16[1536,128]{1,0:T(8,128)(2,1)}, u32[]{:S(2)}, u32[]{:S(2)}) collective-permute-start(bf16[1536,128]{1,0:T(8,128)(2,1)S(1)} %pad_maximum_fusion.2), channel_id=1, source_target_pairs={{24,0},{25,1},{26,2},{27,3},{28,4},{29,5},{30,6},{31,7},{32,8},{33... | collective-permute-start | bytes 1179656 | tf_op jit(solution)/shard_map/ppermute | solution.py:22
  41.5 1.3 %collective-permute-start.2 = (bf16[768,128]{1,0:T(8,128)(2,1)S(1)}, bf16[768,128]{1,0:T(8,128)(2,1)}, u32[]{:S(2)}, u32[]{:S(2)}) collective-permute-start(bf16[768,128]{1,0:T(8,128)(2,1)S(1)} %collective-permute-done), channel_id=1, source_target_pairs={{60,12},{61,13},{62,14},{63,15},{64,16},{65,17},{66,18},{67,19},{6... | collective-permute-start | bytes 589832 | tf_op jit(solution)/shard_map/ppermute | solution.py:22
  42.8 0.6 slice_reduce_fusion
  44.1 4.3 %all-to-all-start.3 = ((bf16[6,256,128]{2,1,0:T(8,128)(2,1)}), bf16[6,256,128]{2,1,0:T(8,128)(2,1)}, u32[]{:S(2)}, u32[]{:S(2)}) async-start(bf16[6,256,128]{2,1,0:T(8,128)(2,1)} %bitcast.14), calls=%async_computation.3 | async-start | bytes 786432 | tf_op jit(solution)/shard_map/all_to_all | solution.py:56
  48.4 1.2 %pad_maximum_fusion.here_ref = bf16[3840,128]{1,0:T(8,128)(2,1)S(1)} fusion(bf16[768,128]{1,0:T(8,128)(2,1)} %collective-permute-done.2, bf16[1536,128]{1,0:T(8,128)(2,1)} %collective-permute-done.1, bf16[768,128]{1,0:T(8,128)(2,1)} %copy-done.6, bf16[768,128]{1,0:T(8,128)(2,1)S(1)} %convert_bitcast_fusion.x_ref), kind=kLoop, calls=%fused_computation | loop fusion | flops 3932160 | bytes 1966080 | tf_op jit(solution)/shard_map/concatenate | solution.py:298
  49.6 4.6 %collective-permute-start.3 = (bf16[3840,128]{1,0:T(8,128)(2,1)S(1)}, bf16[3840,128]{1,0:T(8,128)(2,1)}, u32[]{:S(2)}, u32[]{:S(2)}) collective-permute-start(bf16[3840,128]{1,0:T(8,128)(2,1)S(1)} %pad_maximum_fusion.here_ref), channel_id=1, source_target_pairs={{0,6},{1,7},{2,8},{3,9},{4,10},{5,11},{6,0},{7,1},{8,2},{9,3},{10,... | collective-permute-start | bytes 2949128 | tf_op jit(solution)/shard_map/ppermute | solution.py:22
  54.3 10.9 %all-to-all-done.3 = bf16[6,256,128]{2,1,0:T(8,128)(2,1)} async-done(((bf16[6,256,128]{2,1,0:T(8,128)(2,1)}), bf16[6,256,128]{2,1,0:T(8,128)(2,1)}, u32[]{:S(2)}, u32[]{:S(2)}) %all-to-all-start.3) | async-done | bytes 393248 | tf_op jit(solution)/shard_map/all_to_all | solution.py:56
  65.2 1.9 %shard_map.66 = bf16[528,128]{1,0:T(8,128)(2,1)S(1)} custom-call(s32[64]{0:T(128)S(1)} %copy-done.3, s32[64]{0:T(128)S(1)} %get-tuple-element.47.counts_ref, bf16[1536,128]{1,0:T(8,128)(2,1)} %bitcast.15.first_ref, bf16[1536,128]{1,0:T(8,128)(2,1)} %copy-done.5, bf16[512,128]{1,0:T(8,128)(2,1)S(1)} %get-tuple-element.35.own_ref, ...), custom_call_target="tpu_custom_call" | custom-call | tf_op jit(solution)/shard_map/pallas_call | solution.py:169
  67.1 10.1 %collective-permute-start.4 = (bf16[528,128]{1,0:T(8,128)(2,1)S(1)}, bf16[528,128]{1,0:T(8,128)(2,1)}, u32[]{:S(2)}, u32[]{:S(2)}) collective-permute-start(bf16[528,128]{1,0:T(8,128)(2,1)S(1)} %shard_map.66), channel_id=1, source_target_pairs={{0,12},{1,13},{2,14},{3,15},{4,16},{5,17},{6,18},{7,19},{8,20},{9,... | collective-permute-start | bytes 405512 | tf_op jit(solution)/shard_map/ppermute | solution.py:22
  77.3 3.7 %shard_map.67 = (bf16[1536,128]{1,0:T(8,128)(2,1)}, bf16[1536,128]{1,0:T(8,128)(2,1)}, bf16[512,128]{1,0:T(8,128)(2,1)S(1)}) custom-call(s32[64]{0:T(128)S(1)} %get-tuple-element.46.places_ref, s32[64]{0:T(128)S(1)} %copy-done.3, s32[64]{0:T(128)S(1)} %get-tuple-element.47.counts_ref, bf16[3840,128]{1,0:T(8,128)(2,1)S(1)} %pad_maximum_fusion.here_ref, ...), custom_call_target="tpu_custom_call" | custom-call | tf_op jit(solution)/shard_map/pallas_call | solution.py:205
  81.0 0.9 pad_maximum_fusion.3
  81.9 2.3 %collective-permute-start.5 = (bf16[1056,128]{1,0:T(8,128)(2,1)S(1)}, bf16[1056,128]{1,0:T(8,128)(2,1)S(1)}, u32[]{:S(2)}, u32[]{:S(2)}) collective-permute-start(bf16[1056,128]{1,0:T(8,128)(2,1)S(1)} %pad_maximum_fusion.3), channel_id=1, source_target_pairs={{0,24},{1,25},{2,26},{3,27},{4,28},{5,29},{6,30},{7,31},{8,32},{9,... | collective-permute-start | bytes 811016 | tf_op jit(solution)/shard_map/ppermute | solution.py:22
  84.2 2.0 %collective-permute-start.6 = (bf16[528,128]{1,0:T(8,128)(2,1)}, bf16[528,128]{1,0:T(8,128)(2,1)S(1)}, u32[]{:S(2)}, u32[]{:S(2)}) collective-permute-start(bf16[528,128]{1,0:T(8,128)(2,1)} %collective-permute-done.4), channel_id=1, source_target_pairs={{0,48},{1,49},{2,50},{3,51},{4,52},{5,53},{6,54},{7,55},{8,56},{9,... | collective-permute-start | bytes 405512 | tf_op jit(solution)/shard_map/ppermute | solution.py:22
  86.3 9.0 %all-to-all-start.4 = ((bf16[6,256,128]{2,1,0:T(8,128)(2,1)}), bf16[6,256,128]{2,1,0:T(8,128)(2,1)S(1)}, u32[]{:S(2)}, u32[]{:S(2)}) async-start(bf16[6,256,128]{2,1,0:T(8,128)(2,1)} %bitcast.19), calls=%async_computation.4 | async-start | bytes 786432 | tf_op jit(solution)/shard_map/all_to_all | solution.py:56
  95.8 1.0 pad_maximum_fusion.1.refs_0_
  96.8 7.2 %collective-permute-start.7 = (bf16[2640,128]{1,0:T(8,128)(2,1)S(1)}, bf16[2640,128]{1,0:T(8,128)(2,1)S(1)}, u32[]{:S(2)}, u32[]{:S(2)}) collective-permute-start(bf16[2640,128]{1,0:T(8,128)(2,1)S(1)} %pad_maximum_fusion.1.refs_0_), channel_id=1, source_target_pairs={{0,6},{1,7},{2,8},{3,9},{4,10},{5,11},{6,0},{7,1},{8,2},{9,3},{10,... | collective-permute-start | bytes 2027528 | tf_op jit(solution)/shard_map/ppermute | solution.py:22
  104.0 1.7 %collective-permute-done.7.refs_1_ = bf16[2640,128]{1,0:T(8,128)(2,1)S(1)} collective-permute-done((bf16[2640,128]{1,0:T(8,128)(2,1)S(1)}, bf16[2640,128]{1,0:T(8,128)(2,1)S(1)}, u32[]{:S(2)}, u32[]{:S(2)}) %collective-permute-start.7) | collective-permute-done | bytes 675872 | tf_op jit(solution)/shard_map/ppermute | solution.py:22
  105.8 6.3 %all-to-all-done.4 = bf16[6,256,128]{2,1,0:T(8,128)(2,1)S(1)} async-done(((bf16[6,256,128]{2,1,0:T(8,128)(2,1)}), bf16[6,256,128]{2,1,0:T(8,128)(2,1)S(1)}, u32[]{:S(2)}, u32[]{:S(2)}) %all-to-all-start.4) | async-done | bytes 393248 | tf_op jit(solution)/shard_map/all_to_all | solution.py:56
  112.0 3.0 %shard_map.68 = f32[768,128]{1,0:T(8,128)} custom-call(s32[3]{0:T(128)S(1)} %copy-done.2, s32[1]{0:T(128)} %bitcast.7.most_ref, s32[6,8,128]{2,1,0:T(8,128)S(1)} %all_to_all.25.asked_ref, bf16[1536,128]{1,0:T(8,128)(2,1)S(1)} %bitcast.31, bf16[1536,128]{1,0:T(8,128)(2,1)S(1)} %copy-done.4, bf16[512,128]{1,0:T(8,128)(2,1)S(1)} %get-tuple-element.41.own_ref, ...), custom_call_target="tpu_custom_call" | custom-call | tf_op jit(solution)/shard_map/pallas_call | solution.py:254
  (31 shorter events, 1.8 us)
Async XLA Ops:
  1.0 35.1 %collective-permute-start = (bf16[768,128]{1,0:T(8,128)(2,1)S(1)}, bf16[768,128]{1,0:T(8,128)(2,1)S(1)}, u32[]{:S(2)}, u32[]{:S(2)}) collective-permute-start(bf16[768,128]{1,0:T(8,128)(2,1)S(1)} %convert_bitcast_fusion.x_ref), channel_id=1, source_target_pairs={{0,12},{1,13},{2,14},{3,15},{4,16},{5,17},{6,18},{7,19},{8,20},{9,... | collective-permute-start | bytes 589832 | tf_op jit(solution)/shard_map/ppermute | solution.py:22
  33.6 0.6 copy-start.1
  36.1 12.3 %copy-start.6 = (bf16[768,128]{1,0:T(8,128)(2,1)}, bf16[768,128]{1,0:T(8,128)(2,1)S(1)}, u32[]{:S(2)}) copy-start(bf16[768,128]{1,0:T(8,128)(2,1)S(1)} %collective-permute-done) | copy-start | bytes 589828
  36.1 12.3 %collective-permute-start.1 = (bf16[1536,128]{1,0:T(8,128)(2,1)S(1)}, bf16[1536,128]{1,0:T(8,128)(2,1)}, u32[]{:S(2)}, u32[]{:S(2)}) collective-permute-start(bf16[1536,128]{1,0:T(8,128)(2,1)S(1)} %pad_maximum_fusion.2), channel_id=1, source_target_pairs={{24,0},{25,1},{26,2},{27,3},{28,4},{29,5},{30,6},{31,7},{32,8},{33... | collective-permute-start | bytes 1179656 | tf_op jit(solution)/shard_map/ppermute | solution.py:22
  41.5 6.9 %collective-permute-start.2 = (bf16[768,128]{1,0:T(8,128)(2,1)S(1)}, bf16[768,128]{1,0:T(8,128)(2,1)}, u32[]{:S(2)}, u32[]{:S(2)}) collective-permute-start(bf16[768,128]{1,0:T(8,128)(2,1)S(1)} %collective-permute-done), channel_id=1, source_target_pairs={{60,12},{61,13},{62,14},{63,15},{64,16},{65,17},{66,18},{67,19},{6... | collective-permute-start | bytes 589832 | tf_op jit(solution)/shard_map/ppermute | solution.py:22
  44.0 10.2 %copy-start.7 = (s32[64]{0:T(128)S(1)}, s32[64]{0:T(128)}, u32[]{:S(2)}) copy-start(s32[64]{0:T(128)} %param.13) | copy-start | bytes 772
  44.0 10.2 %copy-start.8 = (s32[64]{0:T(128)S(1)}, s32[64]{0:T(128)}, u32[]{:S(2)}) copy-start(s32[64]{0:T(128)} %param.14) | copy-start | bytes 772
  44.0 21.1 %copy-start = (bf16[64,128,128]{2,1,0:T(8,128)(2,1)S(1)}, bf16[64,128,128]{2,1,0:T(8,128)(2,1)}, u32[]{:S(2)}) copy-start(bf16[64,128,128]{2,1,0:T(8,128)(2,1)} %tiles_ref.3) | copy-start | bytes 6291460
  44.1 21.1 %copy-start.3 = (s32[64]{0:T(128)S(1)}, s32[64]{0:T(128)}, u32[]{:S(2)}) copy-start(s32[64]{0:T(128)} %get-tuple-element.30.places_ref.goals_ref) | copy-start | bytes 772
  44.1 4.3 %copy-start.5 = (bf16[1536,128]{1,0:T(8,128)(2,1)}, bf16[1536,128]{1,0:T(8,128)(2,1)S(1)}, u32[]{:S(2)}) copy-start(bf16[1536,128]{1,0:T(8,128)(2,1)S(1)} %get-tuple-element.48.second_ref) | copy-start | bytes 1179652
  44.1 21.1 %all-to-all-start.3 = ((bf16[6,256,128]{2,1,0:T(8,128)(2,1)}), bf16[6,256,128]{2,1,0:T(8,128)(2,1)}, u32[]{:S(2)}, u32[]{:S(2)}) async-start(bf16[6,256,128]{2,1,0:T(8,128)(2,1)} %bitcast.14), calls=%async_computation.3 | async-start | bytes 786432 | tf_op jit(solution)/shard_map/all_to_all | solution.py:56
  49.6 27.6 %collective-permute-start.3 = (bf16[3840,128]{1,0:T(8,128)(2,1)S(1)}, bf16[3840,128]{1,0:T(8,128)(2,1)}, u32[]{:S(2)}, u32[]{:S(2)}) collective-permute-start(bf16[3840,128]{1,0:T(8,128)(2,1)S(1)} %pad_maximum_fusion.here_ref), channel_id=1, source_target_pairs={{0,6},{1,7},{2,8},{3,9},{4,10},{5,11},{6,0},{7,1},{8,2},{9,3},{10,... | collective-permute-start | bytes 2949128 | tf_op jit(solution)/shard_map/ppermute | solution.py:22
  67.1 13.9 %collective-permute-start.4 = (bf16[528,128]{1,0:T(8,128)(2,1)S(1)}, bf16[528,128]{1,0:T(8,128)(2,1)}, u32[]{:S(2)}, u32[]{:S(2)}) collective-permute-start(bf16[528,128]{1,0:T(8,128)(2,1)S(1)} %shard_map.66), channel_id=1, source_target_pairs={{0,12},{1,13},{2,14},{3,15},{4,16},{5,17},{6,18},{7,19},{8,20},{9,... | collective-permute-start | bytes 405512 | tf_op jit(solution)/shard_map/ppermute | solution.py:22
  81.9 30.1 %copy-start.2 = (s32[3]{0:T(128)S(1)}, s32[3]{0:T(128)}, u32[]{:S(2)}) copy-start(s32[3]{0:T(128)} %pad_add_fusion.place_ref) | copy-start | bytes 40
  81.9 13.9 %collective-permute-start.5 = (bf16[1056,128]{1,0:T(8,128)(2,1)S(1)}, bf16[1056,128]{1,0:T(8,128)(2,1)S(1)}, u32[]{:S(2)}, u32[]{:S(2)}) collective-permute-start(bf16[1056,128]{1,0:T(8,128)(2,1)S(1)} %pad_maximum_fusion.3), channel_id=1, source_target_pairs={{0,24},{1,25},{2,26},{3,27},{4,28},{5,29},{6,30},{7,31},{8,32},{9,... | collective-permute-start | bytes 811016 | tf_op jit(solution)/shard_map/ppermute | solution.py:22
  84.2 11.6 %collective-permute-start.6 = (bf16[528,128]{1,0:T(8,128)(2,1)}, bf16[528,128]{1,0:T(8,128)(2,1)S(1)}, u32[]{:S(2)}, u32[]{:S(2)}) collective-permute-start(bf16[528,128]{1,0:T(8,128)(2,1)} %collective-permute-done.4), channel_id=1, source_target_pairs={{0,48},{1,49},{2,50},{3,51},{4,52},{5,53},{6,54},{7,55},{8,56},{9,... | collective-permute-start | bytes 405512 | tf_op jit(solution)/shard_map/ppermute | solution.py:22
  86.3 25.8 %copy-start.4 = (bf16[1536,128]{1,0:T(8,128)(2,1)S(1)}, bf16[1536,128]{1,0:T(8,128)(2,1)}, u32[]{:S(2)}) copy-start(bf16[1536,128]{1,0:T(8,128)(2,1)} %get-tuple-element.49.second_ref) | copy-start | bytes 1179652
  86.3 25.7 %all-to-all-start.4 = ((bf16[6,256,128]{2,1,0:T(8,128)(2,1)}), bf16[6,256,128]{2,1,0:T(8,128)(2,1)S(1)}, u32[]{:S(2)}, u32[]{:S(2)}) async-start(bf16[6,256,128]{2,1,0:T(8,128)(2,1)} %bitcast.19), calls=%async_computation.4 | async-start | bytes 786432 | tf_op jit(solution)/shard_map/all_to_all | solution.py:56
  96.8 9.0 %collective-permute-start.7 = (bf16[2640,128]{1,0:T(8,128)(2,1)S(1)}, bf16[2640,128]{1,0:T(8,128)(2,1)S(1)}, u32[]{:S(2)}, u32[]{:S(2)}) collective-permute-start(bf16[2640,128]{1,0:T(8,128)(2,1)S(1)} %pad_maximum_fusion.1.refs_0_), channel_id=1, source_target_pairs={{0,6},{1,7},{2,8},{3,9},{4,10},{5,11},{6,0},{7,1},{8,2},{9,3},{10,... | collective-permute-start | bytes 2027528 | tf_op jit(solution)/shard_map/ppermute | solution.py:22

commit v4 on v3

--- a/solution.py
+++ b/solution.py
@@ -216,28 +216,8 @@
     )(places, goals, counts, here, there, tiles)
 
 
-def sum_kernel(cols, slots, place_ref, most_ref, asked_ref, first_ref, second_ref, own_ref, *refs):
-    lists, (out_ref, acc) = refs[:-2], refs[-2:]
-    tiles_here = out_ref.shape[0] // 8
+def add_lists(lists, own, slots, acc):
     rows = 8 * slots + LIST_TAIL
-    near = lax.broadcasted_iota(jnp.int32, (tiles_here, LANES), 0)
-    own = (near + place_ref[2]).astype(jnp.float32)
-    acc[...] = jnp.zeros_like(acc)
-
-    def add_forward(ref, askers):
-        chosen = [chosen_of(asked_ref, col, near)[:, start : start + SHARE] for col, start in askers]
-        chosen = jnp.concatenate(chosen, axis=1).astype(jnp.bfloat16)
-        for vec in range(8):
-            values = [ref[(i * 8 + vec) * SHARE : (i * 8 + vec + 1) * SHARE, :] for i in range(len(askers))]
-            acc[vec] += jnp.dot(chosen, jnp.concatenate(values, axis=0), preferred_element_type=jnp.float32)
-
-    add_forward(first_ref, [(col, 0) for col in range(cols)])
-    add_forward(own_ref, [(place_ref[0], 0), (place_ref[0], SHARE)])
-
-    @pl.when(most_ref[0] > SHARE)
-    def _():
-        add_forward(second_ref, [(col, SHARE) for col in range(cols)])
-
     for part in lists:
         for start in range(0, part.shape[0], rows):
             digits = part[start + 8 * slots : start + rows, :].astype(jnp.float32)
@@ -246,19 +226,64 @@
             for vec in range(8):
                 values = part[start + vec * slots : start + (vec + 1) * slots, :]
                 acc[vec] += jnp.dot(chosen, values, preferred_element_type=jnp.float32)
+
+
+def own_tiles(place_ref, tiles_here):
+    return (lax.broadcasted_iota(jnp.int32, (tiles_here, LANES), 0) + place_ref[2]).astype(jnp.float32)
+
+
+def first_sum_kernel(cols, slots, place_ref, most_ref, asked_ref, first_ref, second_ref, own_ref, list_ref, acc):
+    tiles_here = acc.shape[1]
+    near = lax.broadcasted_iota(jnp.int32, (tiles_here, LANES), 0)
+    acc[...] = jnp.zeros_like(acc)
+
+    def add_forward(ref, askers):
+        chosen = [chosen_of(asked_ref, col, near)[:, start : start + SHARE] for col, start in askers]
+        chosen = jnp.concatenate(chosen, axis=1).astype(jnp.bfloat16)
+        for vec in range(8):
+            values = [ref[(i * 8 + vec) * SHARE : (i * 8 + vec + 1) * SHARE, :] for i in range(len(askers))]
+            acc[vec] += jnp.dot(chosen, jnp.concatenate(values, axis=0), preferred_element_type=jnp.float32)
+
+    add_forward(first_ref, [(col, 0) for col in range(cols)])
+    add_forward(own_ref, [(place_ref[0], 0), (place_ref[0], SHARE)])
+
+    @pl.when(most_ref[0] > SHARE)
+    def _():
+        add_forward(second_ref, [(col, SHARE) for col in range(cols)])
+
+    add_lists([list_ref], own_tiles(place_ref, tiles_here), slots, acc)
+
+
+def first_sum(place, most, asked, first, second, own, some, slots, cols, tiles_here):
+    return pl.pallas_call(
+        functools.partial(first_sum_kernel, cols, slots),
+        out_shape=jax.ShapeDtypeStruct((8, tiles_here, LANES), jnp.float32),
+        in_specs=[SMEM, SMEM] + [VMEM] * 5,
+        out_specs=VMEM,
+        compiler_params=PARAMS,
+        cost_estimate=LITTLE,
+    )(place, most, asked, first, second, own, some)
+
+
+def last_sum_kernel(slots, place_ref, start_ref, list_ref, out_ref, acc):
+    tiles_here = acc.shape[1]
+    acc[...] = start_ref[...]
+    add_lists([list_ref], own_tiles(place_ref, tiles_here), slots, acc)
     for vec in range(8):
         out_ref[pl.ds(vec, tiles_here, stride=8), :] = acc[vec]
 
 
-def summed(place, most, asked, first, second, own, lists, slots, cols, tiles_here):
-    return pl.pallas_call(
-        functools.partial(sum_kernel, cols, slots),
+def last_sum(place, start, some, slots):
+    tiles_here = start.shape[1]
+    return pl.pallas_call(
+        functools.partial(last_sum_kernel, slots),
         out_shape=jax.ShapeDtypeStruct((8 * tiles_here, LANES), jnp.float32),
-        in_specs=[SMEM, SMEM] + [VMEM] * (4 + len(lists)),
+        in_specs=[SMEM, VMEM, VMEM],
         out_specs=VMEM,
-        scratch_shapes=[pltpu.VMEM((8, tiles_here, LANES), jnp.float32)],
-        compiler_params=PARAMS,
-    )(place, most, asked, first, second, own, *lists)
+        scratch_shapes=[pltpu.VMEM(start.shape, jnp.float32)],
+        compiler_params=PARAMS,
+        cost_estimate=LITTLE,
+    )(place, start, some)
 
 
 def tail_of(ids):
@@ -303,12 +328,14 @@
     forward, late_forward, own_forward = forward_products(col_places, row_places, counts, here, there, tiles, cols)
     mirror_both = join([mirror, after(mirror_across, forward)])
     mirror_groups = next_groups(mirror_both, *grid, 1)
-    forward = over_columns(after(forward, mirror_both), cols)
+    forward = over_columns(forward, cols)
     late_forward = lax.cond(most > SHARE, lambda v: over_columns(v, cols), lambda v: v, late_forward)
-    mirror_here = after(join([mirror_both, *mirror_groups]), late_forward)
+    mirror_here = after(join([mirror_both, *mirror_groups]), late_forward, forward)
     mirror_there = other_core(mirror_here, *grid)
-    lists = [mirror_here, mirror_there]
-    total = summed(place, most.reshape(1), asked, forward, late_forward, own_forward, lists, slots, cols, per_piece)
+    partial = first_sum(
+        place, most.reshape(1), asked, forward, late_forward, own_forward, mirror_here, slots, cols, per_piece
+    )
+    total = last_sum(place, partial, mirror_there, slots)
     return total.reshape(per_piece, vec_count, tile_len).transpose(1, 0, 2).reshape(vec_count, seg_len)
 
 

time: 117 us -> 111 us (0.949)
  starting transfers between devices: 61.1 us -> 54 us
    ppermute x8, waiting for transfers between devices: 2.25 us -> 8.34 us  [send(): return lax.ppermute(value, AXES, moves)]
    all_to_all x2, waiting for transfers between devices: 17.2 us -> 11.6 us  [over_columns(): lax.all_to_all(value.reshape(cols, -1, LANES), 'col', 0, 0)]
    all_to_all x2, starting transfers between devices: 13.3 us -> 7.86 us  [over_columns(): lax.all_to_all(value.reshape(cols, -1, LANES), 'col', 0, 0)]
    ppermute x8, starting transfers between devices: 47.8 us -> 46.1 us  [send(): return lax.ppermute(value, AXES, moves)]
    pallas_call x1 -> x2, Pallas kernels: 3 us -> 3.78 us  [the longest x1 2.08 us: first_sum(): pl.pallas_call(functools.partial(first_sum_kernel, cols, slots), out_shap...]
  transfers between devices with their start and end apart: 10 -> 10, of which waited for: 4 -> 3; matrix products, arithmetic and copies ran while one was open for 3% -> 4% of each run, Pallas kernels for 9% -> 11%
where the time goes in v4:
time: 111 us; the launch traced here: 110 us
  starting transfers between devices  54 us (49%)
  waiting for transfers between devices  19.9 us (18%)
  Pallas kernels  14 us (13%)
  blocking collectives  13.6 us (12%)
  other arithmetic  5.47 us (5%)
  between operations  1.63 us (1%)
  local copies, waits for them, and re-layouts  1.38 us (1%)
    ppermute x8, starting transfers between devices, send(): return lax.ppermute(value, AXES, moves)  46.1 us
    all_to_all x1, blocking collectives, local(): asked = lax.all_to_all(wanted, 'col', 0, 0)  13.6 us
    all_to_all x2, waiting for transfers between devices, over_columns(): lax.all_to_all(value.reshape(cols, -1, LANES), 'col', 0, 0)  11.6 us
    ppermute x8, waiting for transfers between devices, send(): return lax.ppermute(value, AXES, moves)  8.34 us
    all_to_all x2, starting transfers between devices, over_columns(): lax.all_to_all(value.reshape(cols, -1, LANES), 'col', 0, 0)  7.86 us
    pallas_call x1, Pallas kernels, forward_products(): pl.pallas_call(forward_kernel, out_shape=(shape, shape, own), in_specs=[S...  3.63 us
    pallas_call x1, Pallas kernels, requests(): pl.pallas_call(functools.partial(request_kernel, cols, per_piece), out_sh...  2.8 us
  transfers between devices with their start and end apart: 10, of which 3 were waited for; matrix products, arithmetic and copies ran while one was open for 4% of the time, Pallas kernels for 11%

profile of v4, /device:TPU:7, one launch (start us, length us, event | category | flops | bytes accessed | tf_op | source)
XLA Modules:
  0.0 110.0 jit_solution(7120632065088271174)
XLA Ops:
  0.0 1.0 convert_bitcast_fusion.x_ref
  1.0 14.9 %collective-permute-start = (bf16[768,128]{1,0:T(8,128)(2,1)S(1)}, bf16[768,128]{1,0:T(8,128)(2,1)S(1)}, u32[]{:S(2)}, u32[]{:S(2)}) collective-permute-start(bf16[768,128]{1,0:T(8,128)(2,1)S(1)} %convert_bitcast_fusion.x_ref), channel_id=1, source_target_pairs={{0,12},{1,13},{2,14},{3,15},{4,16},{5,17},{6,18},{7,19},{8,20},{9,... | collective-permute-start | bytes 589832 | tf_op jit(solution)/shard_map/ppermute | solution.py:22
  17.1 2.8 %shard_map.64 = (s32[6,8,128]{2,1,0:T(8,128)}, s32[64]{0:T(128)}) custom-call(s32[3]{0:T(128)} %pad_add_fusion.place_ref, s32[64]{0:T(128)} %rows_ref.1, s32[1]{0:T(128)} %copy.11.live_ref), custom_call_target="tpu_custom_call" | custom-call | tf_op jit(solution)/shard_map/pallas_call | solution.py:96
  19.9 13.6 %all_to_all.25.asked_ref = s32[6,8,128]{2,1,0:T(8,128)S(1)} all-to-all(s32[6,8,128]{2,1,0:T(8,128)} %get-tuple-element.28), channel_id=1, replica_groups=mesh['row'=128,'col'=6] {'col'}, dimensions={0} | all-to-all | bytes 49152 | tf_op jit(solution)/shard_map/all_to_all | solution.py:316
  34.2 1.9 %shard_map.65 = (bf16[1536,128]{1,0:T(8,128)(2,1)}, bf16[1536,128]{1,0:T(8,128)(2,1)S(1)}, bf16[512,128]{1,0:T(8,128)(2,1)S(1)}) custom-call(s32[3]{0:T(128)S(1)} %copy-done.2, s32[6,8,128]{2,1,0:T(8,128)S(1)} %all_to_all.25.asked_ref, bf16[768,128]{1,0:T(8,128)(2,1)S(1)} %convert_bitcast_fusion.x_ref), custom_call_target="tpu_custom_call" | custom-call | tf_op jit(solution)/shard_map/pallas_call | solution.py:139
  36.1 5.4 %collective-permute-start.1 = (bf16[1536,128]{1,0:T(8,128)(2,1)S(1)}, bf16[1536,128]{1,0:T(8,128)(2,1)}, u32[]{:S(2)}, u32[]{:S(2)}) collective-permute-start(bf16[1536,128]{1,0:T(8,128)(2,1)S(1)} %pad_maximum_fusion.2), channel_id=1, source_target_pairs={{24,0},{25,1},{26,2},{27,3},{28,4},{29,5},{30,6},{31,7},{32,8},{33... | collective-permute-start | bytes 1179656 | tf_op jit(solution)/shard_map/ppermute | solution.py:22
  41.4 1.4 %collective-permute-start.2 = (bf16[768,128]{1,0:T(8,128)(2,1)S(1)}, bf16[768,128]{1,0:T(8,128)(2,1)}, u32[]{:S(2)}, u32[]{:S(2)}) collective-permute-start(bf16[768,128]{1,0:T(8,128)(2,1)S(1)} %collective-permute-done), channel_id=1, source_target_pairs={{60,12},{61,13},{62,14},{63,15},{64,16},{65,17},{66,18},{67,19},{6... | collective-permute-start | bytes 589832 | tf_op jit(solution)/shard_map/ppermute | solution.py:22
  44.3 4.3 %all-to-all-start.3 = ((bf16[6,256,128]{2,1,0:T(8,128)(2,1)}), bf16[6,256,128]{2,1,0:T(8,128)(2,1)}, u32[]{:S(2)}, u32[]{:S(2)}) async-start(bf16[6,256,128]{2,1,0:T(8,128)(2,1)} %bitcast.14), calls=%async_computation.3 | async-start | bytes 786432 | tf_op jit(solution)/shard_map/all_to_all | solution.py:56
  48.6 1.2 %pad_maximum_fusion.here_ref = bf16[3840,128]{1,0:T(8,128)(2,1)S(1)} fusion(bf16[768,128]{1,0:T(8,128)(2,1)} %collective-permute-done.2, bf16[1536,128]{1,0:T(8,128)(2,1)} %collective-permute-done.1, bf16[768,128]{1,0:T(8,128)(2,1)} %copy-done.7, bf16[768,128]{1,0:T(8,128)(2,1)S(1)} %convert_bitcast_fusion.x_ref), kind=kLoop, calls=%fused_computation | loop fusion | flops 3932160 | bytes 1966080 | tf_op jit(solution)/shard_map/concatenate | solution.py:323
  49.8 4.6 %collective-permute-start.3 = (bf16[3840,128]{1,0:T(8,128)(2,1)S(1)}, bf16[3840,128]{1,0:T(8,128)(2,1)}, u32[]{:S(2)}, u32[]{:S(2)}) collective-permute-start(bf16[3840,128]{1,0:T(8,128)(2,1)S(1)} %pad_maximum_fusion.here_ref), channel_id=1, source_target_pairs={{0,6},{1,7},{2,8},{3,9},{4,10},{5,11},{6,0},{7,1},{8,2},{9,3},{10,... | collective-permute-start | bytes 2949128 | tf_op jit(solution)/shard_map/ppermute | solution.py:22
  54.5 10.9 %all-to-all-done.3 = bf16[6,256,128]{2,1,0:T(8,128)(2,1)} async-done(((bf16[6,256,128]{2,1,0:T(8,128)(2,1)}), bf16[6,256,128]{2,1,0:T(8,128)(2,1)}, u32[]{:S(2)}, u32[]{:S(2)}) %all-to-all-start.3) | async-done | bytes 393248 | tf_op jit(solution)/shard_map/all_to_all | solution.py:56
  65.3 1.9 %shard_map.66 = bf16[528,128]{1,0:T(8,128)(2,1)S(1)} custom-call(s32[64]{0:T(128)S(1)} %copy-done.4, s32[64]{0:T(128)S(1)} %get-tuple-element.45.counts_ref, bf16[1536,128]{1,0:T(8,128)(2,1)} %bitcast.15.first_ref, bf16[1536,128]{1,0:T(8,128)(2,1)} %copy-done.6, bf16[512,128]{1,0:T(8,128)(2,1)S(1)} %get-tuple-element.34.own_ref, ...), custom_call_target="tpu_custom_call" | custom-call | tf_op jit(solution)/shard_map/pallas_call | solution.py:169
  67.3 8.8 %collective-permute-start.4 = (bf16[528,128]{1,0:T(8,128)(2,1)S(1)}, bf16[528,128]{1,0:T(8,128)(2,1)}, u32[]{:S(2)}, u32[]{:S(2)}) collective-permute-start(bf16[528,128]{1,0:T(8,128)(2,1)S(1)} %shard_map.66), channel_id=1, source_target_pairs={{0,12},{1,13},{2,14},{3,15},{4,16},{5,17},{6,18},{7,19},{8,20},{9,... | collective-permute-start | bytes 405512 | tf_op jit(solution)/shard_map/ppermute | solution.py:22
  76.1 3.6 %shard_map.67 = (bf16[1536,128]{1,0:T(8,128)(2,1)S(1)}, bf16[1536,128]{1,0:T(8,128)(2,1)}, bf16[512,128]{1,0:T(8,128)(2,1)S(1)}) custom-call(s32[64]{0:T(128)S(1)} %get-tuple-element.44.places_ref, s32[64]{0:T(128)S(1)} %copy-done.4, s32[64]{0:T(128)S(1)} %get-tuple-element.45.counts_ref, bf16[3840,128]{1,0:T(8,128)(2,1)S(1)} %pad_maximum_fusion.here_ref, ...), custom_call_target="tpu_custom_call" | custom-call | tf_op jit(solution)/shard_map/pallas_call | solution.py:205
  79.7 0.7 copy-done.1
  80.4 3.6 %all-to-all-start.4 = ((bf16[6,256,128]{2,1,0:T(8,128)(2,1)}), bf16[6,256,128]{2,1,0:T(8,128)(2,1)S(1)}, u32[]{:S(2)}, u32[]{:S(2)}) async-start(bf16[6,256,128]{2,1,0:T(8,128)(2,1)} %bitcast.32), calls=%async_computation.4 | async-start | bytes 786432 | tf_op jit(solution)/shard_map/all_to_all | solution.py:56
  84.1 0.9 pad_maximum_fusion.3
  85.0 2.3 %collective-permute-start.5 = (bf16[1056,128]{1,0:T(8,128)(2,1)S(1)}, bf16[1056,128]{1,0:T(8,128)(2,1)S(1)}, u32[]{:S(2)}, u32[]{:S(2)}) collective-permute-start(bf16[1056,128]{1,0:T(8,128)(2,1)S(1)} %pad_maximum_fusion.3), channel_id=1, source_target_pairs={{0,24},{1,25},{2,26},{3,27},{4,28},{5,29},{6,30},{7,31},{8,32},{9,... | collective-permute-start | bytes 811016 | tf_op jit(solution)/shard_map/ppermute | solution.py:22
  87.3 3.5 %collective-permute-start.6 = (bf16[528,128]{1,0:T(8,128)(2,1)}, bf16[528,128]{1,0:T(8,128)(2,1)S(1)}, u32[]{:S(2)}, u32[]{:S(2)}) collective-permute-start(bf16[528,128]{1,0:T(8,128)(2,1)} %collective-permute-done.4), channel_id=1, source_target_pairs={{0,48},{1,49},{2,50},{3,51},{4,52},{5,53},{6,54},{7,55},{8,56},{9,... | collective-permute-start | bytes 405512 | tf_op jit(solution)/shard_map/ppermute | solution.py:22
  90.8 8.3 %collective-permute-done.6 = bf16[528,128]{1,0:T(8,128)(2,1)S(1)} collective-permute-done((bf16[528,128]{1,0:T(8,128)(2,1)}, bf16[528,128]{1,0:T(8,128)(2,1)S(1)}, u32[]{:S(2)}, u32[]{:S(2)}) %collective-permute-start.6) | collective-permute-done | bytes 135200 | tf_op jit(solution)/shard_map/ppermute | solution.py:22
  99.1 1.0 pad_maximum_fusion.1.list_ref
  100.8 5.4 %collective-permute-start.7 = (bf16[2640,128]{1,0:T(8,128)(2,1)S(1)}, bf16[2640,128]{1,0:T(8,128)(2,1)S(1)}, u32[]{:S(2)}, u32[]{:S(2)}) collective-permute-start(bf16[2640,128]{1,0:T(8,128)(2,1)S(1)} %pad_maximum_fusion.1.list_ref), channel_id=1, source_target_pairs={{0,6},{1,7},{2,8},{3,9},{4,10},{5,11},{6,0},{7,1},{8,2},{9,3},{10,... | collective-permute-start | bytes 2027528 | tf_op jit(solution)/shard_map/ppermute | solution.py:22
  106.2 2.1 %shard_map.68.start_ref = f32[8,96,128]{2,1,0:T(8,128)S(1)} custom-call(s32[3]{0:T(128)S(1)} %copy-done.3, s32[1]{0:T(128)} %bitcast.7.most_ref, s32[6,8,128]{2,1,0:T(8,128)S(1)} %all_to_all.25.asked_ref, bf16[1536,128]{1,0:T(8,128)(2,1)S(1)} %bitcast.31, bf16[1536,128]{1,0:T(8,128)(2,1)S(1)} %copy-done.5, bf16[512,128]{1,0:T(8,128)(2,1)S(1)} %get-tuple-element.38.own_ref, ...), custom_call_target="tpu_custom_call" | custom-call | tf_op jit(solution)/shard_map/pallas_call | solution.py:258
  108.3 1.7 %shard_map.69 = f32[768,128]{1,0:T(8,128)} custom-call(s32[3]{0:T(128)S(1)} %copy-done.3, f32[8,96,128]{2,1,0:T(8,128)S(1)} %shard_map.68.start_ref, bf16[2640,128]{1,0:T(8,128)(2,1)S(1)} %collective-permute-done.7.list_ref), custom_call_target="tpu_custom_call" | custom-call | tf_op jit(solution)/shard_map/pallas_call | solution.py:278
  (34 shorter events, 2.7 us)
Async XLA Ops:
  1.0 35.0 %collective-permute-start = (bf16[768,128]{1,0:T(8,128)(2,1)S(1)}, bf16[768,128]{1,0:T(8,128)(2,1)S(1)}, u32[]{:S(2)}, u32[]{:S(2)}) collective-permute-start(bf16[768,128]{1,0:T(8,128)(2,1)S(1)} %convert_bitcast_fusion.x_ref), channel_id=1, source_target_pairs={{0,12},{1,13},{2,14},{3,15},{4,16},{5,17},{6,18},{7,19},{8,20},{9,... | collective-permute-start | bytes 589832 | tf_op jit(solution)/shard_map/ppermute | solution.py:22
  33.6 0.6 copy-start.2
  36.0 12.5 %copy-start.7 = (bf16[768,128]{1,0:T(8,128)(2,1)}, bf16[768,128]{1,0:T(8,128)(2,1)S(1)}, u32[]{:S(2)}) copy-start(bf16[768,128]{1,0:T(8,128)(2,1)S(1)} %collective-permute-done) | copy-start | bytes 589828
  36.1 12.5 %collective-permute-start.1 = (bf16[1536,128]{1,0:T(8,128)(2,1)S(1)}, bf16[1536,128]{1,0:T(8,128)(2,1)}, u32[]{:S(2)}, u32[]{:S(2)}) collective-permute-start(bf16[1536,128]{1,0:T(8,128)(2,1)S(1)} %pad_maximum_fusion.2), channel_id=1, source_target_pairs={{24,0},{25,1},{26,2},{27,3},{28,4},{29,5},{30,6},{31,7},{32,8},{33... | collective-permute-start | bytes 1179656 | tf_op jit(solution)/shard_map/ppermute | solution.py:22
  41.4 7.1 %collective-permute-start.2 = (bf16[768,128]{1,0:T(8,128)(2,1)S(1)}, bf16[768,128]{1,0:T(8,128)(2,1)}, u32[]{:S(2)}, u32[]{:S(2)}) collective-permute-start(bf16[768,128]{1,0:T(8,128)(2,1)S(1)} %collective-permute-done), channel_id=1, source_target_pairs={{60,12},{61,13},{62,14},{63,15},{64,16},{65,17},{66,18},{67,19},{6... | collective-permute-start | bytes 589832 | tf_op jit(solution)/shard_map/ppermute | solution.py:22
  44.2 10.2 %copy-start.8 = (s32[64]{0:T(128)S(1)}, s32[64]{0:T(128)}, u32[]{:S(2)}) copy-start(s32[64]{0:T(128)} %param.13) | copy-start | bytes 772
  44.2 10.2 %copy-start.9 = (s32[64]{0:T(128)S(1)}, s32[64]{0:T(128)}, u32[]{:S(2)}) copy-start(s32[64]{0:T(128)} %param.14) | copy-start | bytes 772
  44.2 21.1 %copy-start = (bf16[64,128,128]{2,1,0:T(8,128)(2,1)S(1)}, bf16[64,128,128]{2,1,0:T(8,128)(2,1)}, u32[]{:S(2)}) copy-start(bf16[64,128,128]{2,1,0:T(8,128)(2,1)} %tiles_ref.3) | copy-start | bytes 6291460
  44.2 21.1 %copy-start.4 = (s32[64]{0:T(128)S(1)}, s32[64]{0:T(128)}, u32[]{:S(2)}) copy-start(s32[64]{0:T(128)} %get-tuple-element.29.places_ref.goals_ref) | copy-start | bytes 772
  44.3 4.3 %copy-start.6 = (bf16[1536,128]{1,0:T(8,128)(2,1)}, bf16[1536,128]{1,0:T(8,128)(2,1)S(1)}, u32[]{:S(2)}) copy-start(bf16[1536,128]{1,0:T(8,128)(2,1)S(1)} %get-tuple-element.46.second_ref) | copy-start | bytes 1179652
  44.3 21.1 %all-to-all-start.3 = ((bf16[6,256,128]{2,1,0:T(8,128)(2,1)}), bf16[6,256,128]{2,1,0:T(8,128)(2,1)}, u32[]{:S(2)}, u32[]{:S(2)}) async-start(bf16[6,256,128]{2,1,0:T(8,128)(2,1)} %bitcast.14), calls=%async_computation.3 | async-start | bytes 786432 | tf_op jit(solution)/shard_map/all_to_all | solution.py:56
  49.8 26.3 %collective-permute-start.3 = (bf16[3840,128]{1,0:T(8,128)(2,1)S(1)}, bf16[3840,128]{1,0:T(8,128)(2,1)}, u32[]{:S(2)}, u32[]{:S(2)}) collective-permute-start(bf16[3840,128]{1,0:T(8,128)(2,1)S(1)} %pad_maximum_fusion.here_ref), channel_id=1, source_target_pairs={{0,6},{1,7},{2,8},{3,9},{4,10},{5,11},{6,0},{7,1},{8,2},{9,3},{10,... | collective-permute-start | bytes 2949128 | tf_op jit(solution)/shard_map/ppermute | solution.py:22
  67.3 16.8 %collective-permute-start.4 = (bf16[528,128]{1,0:T(8,128)(2,1)S(1)}, bf16[528,128]{1,0:T(8,128)(2,1)}, u32[]{:S(2)}, u32[]{:S(2)}) collective-permute-start(bf16[528,128]{1,0:T(8,128)(2,1)S(1)} %shard_map.66), channel_id=1, source_target_pairs={{0,12},{1,13},{2,14},{3,15},{4,16},{5,17},{6,18},{7,19},{8,20},{9,... | collective-permute-start | bytes 405512 | tf_op jit(solution)/shard_map/ppermute | solution.py:22
  79.7 0.7 copy-start.1
  80.4 25.8 %copy-start.3 = (s32[3]{0:T(128)S(1)}, s32[3]{0:T(128)}, u32[]{:S(2)}) copy-start(s32[3]{0:T(128)} %pad_add_fusion.place_ref) | copy-start | bytes 40
  80.4 25.8 %copy-start.5 = (bf16[1536,128]{1,0:T(8,128)(2,1)S(1)}, bf16[1536,128]{1,0:T(8,128)(2,1)}, u32[]{:S(2)}) copy-start(bf16[1536,128]{1,0:T(8,128)(2,1)} %get-tuple-element.47.second_ref) | copy-start | bytes 1179652
  80.4 20.3 %all-to-all-start.4 = ((bf16[6,256,128]{2,1,0:T(8,128)(2,1)}), bf16[6,256,128]{2,1,0:T(8,128)(2,1)S(1)}, u32[]{:S(2)}, u32[]{:S(2)}) async-start(bf16[6,256,128]{2,1,0:T(8,128)(2,1)} %bitcast.32), calls=%async_computation.4 | async-start | bytes 786432 | tf_op jit(solution)/shard_map/all_to_all | solution.py:56
  85.0 14.1 %collective-permute-start.5 = (bf16[1056,128]{1,0:T(8,128)(2,1)S(1)}, bf16[1056,128]{1,0:T(8,128)(2,1)S(1)}, u32[]{:S(2)}, u32[]{:S(2)}) collective-permute-start(bf16[1056,128]{1,0:T(8,128)(2,1)S(1)} %pad_maximum_fusion.3), channel_id=1, source_target_pairs={{0,24},{1,25},{2,26},{3,27},{4,28},{5,29},{6,30},{7,31},{8,32},{9,... | collective-permute-start | bytes 811016 | tf_op jit(solution)/shard_map/ppermute | solution.py:22
  87.3 11.8 %collective-permute-start.6 = (bf16[528,128]{1,0:T(8,128)(2,1)}, bf16[528,128]{1,0:T(8,128)(2,1)S(1)}, u32[]{:S(2)}, u32[]{:S(2)}) collective-permute-start(bf16[528,128]{1,0:T(8,128)(2,1)} %collective-permute-done.4), channel_id=1, source_target_pairs={{0,48},{1,49},{2,50},{3,51},{4,52},{5,53},{6,54},{7,55},{8,56},{9,... | collective-permute-start | bytes 405512 | tf_op jit(solution)/shard_map/ppermute | solution.py:22
  100.8 7.6 %collective-permute-start.7 = (bf16[2640,128]{1,0:T(8,128)(2,1)S(1)}, bf16[2640,128]{1,0:T(8,128)(2,1)S(1)}, u32[]{:S(2)}, u32[]{:S(2)}) collective-permute-start(bf16[2640,128]{1,0:T(8,128)(2,1)S(1)} %pad_maximum_fusion.1.list_ref), channel_id=1, source_target_pairs={{0,6},{1,7},{2,8},{3,9},{4,10},{5,11},{6,0},{7,1},{8,2},{9,3},{10,... | collective-permute-start | bytes 2027528 | tf_op jit(solution)/shard_map/ppermute | solution.py:22

commit v5 on v4

--- a/solution.py
+++ b/solution.py
@@ -180,16 +180,19 @@
     )(places, counts, first, second, own, tiles, tail)
 
 
-def forward_kernel(places_ref, goals_ref, counts_ref, here_ref, there_ref, tiles_ref, first_ref, second_ref, own_ref, wide, sums):
+def forward_kernel(places_ref, goals_ref, counts_ref, here_ref, there_ref, tiles_ref, first_ref, second_ref, own_ref, sums):
     slots = tiles_ref.shape[0]
-    half = here_ref.shape[0]
+    half = here_ref.shape[0] // 8
     part = first_ref.shape[0]
-    wide[:half, :] = here_ref[...].astype(jnp.float32)
-    wide[half:, :] = there_ref[...].astype(jnp.float32)
     sums[...] = jnp.zeros_like(sums)
     lanes = lax.broadcasted_iota(jnp.int32, (8, LANES), 1)
     for slot in range(slots):
-        x = wide[pl.ds(pl.multiple_of(places_ref[slot] * 8, 8), 8), :].astype(jnp.bfloat16)
+        place = places_ref[slot]
+        near = place < half
+        place = jnp.where(near, place, place - half)
+        rows = pl.ds(pl.multiple_of(lax.shift_right_logical(place, 1) * 16, 16), 16)
+        pair = jnp.where(near, here_ref[rows, :].astype(jnp.float32), there_ref[rows, :].astype(jnp.float32))
+        x = jnp.where((place & 1) == 0, pair[:8], pair[8:]).astype(jnp.bfloat16)
         y = lax.dot_general(x, tiles_ref[slot], (((1,), (1,)), ((), ())), preferred_element_type=jnp.float32)
         y = jnp.where(lanes < counts_ref[slot], y, 0.0)
         sums[pl.ds(goals_ref[slot], 8, stride=SHARE), :] += y
@@ -208,7 +211,6 @@
         in_specs=[SMEM, SMEM, SMEM, VMEM, VMEM, VMEM],
         out_specs=(VMEM, VMEM, VMEM),
         scratch_shapes=[
-            pltpu.VMEM((2 * here.shape[0], LANES), jnp.float32),
             pltpu.VMEM((2 * part + 3 * 8 * SHARE, LANES), jnp.float32),
         ],
         compiler_params=PARAMS,

time: 111 us -> 111 us (level)
  no operation moved by 1% of the time
where the time goes in v5:
time: 111 us; the launch traced here: 110 us
  starting transfers between devices  54.9 us (49%)
  waiting for transfers between devices  19.6 us (18%)
  Pallas kernels  13.7 us (12%)
  blocking collectives  13.6 us (12%)
  other arithmetic  5.47 us (5%)
  between operations  1.63 us (1%)
  local copies, waits for them, and re-layouts  1.38 us (1%)
    ppermute x8, starting transfers between devices, send(): return lax.ppermute(value, AXES, moves)  47.1 us
    all_to_all x1, blocking collectives, local(): asked = lax.all_to_all(wanted, 'col', 0, 0)  13.6 us
    all_to_all x2, waiting for transfers between devices, over_columns(): lax.all_to_all(value.reshape(cols, -1, LANES), 'col', 0, 0)  11.8 us
    all_to_all x2, starting transfers between devices, over_columns(): lax.all_to_all(value.reshape(cols, -1, LANES), 'col', 0, 0)  7.86 us
    ppermute x8, waiting for transfers between devices, send(): return lax.ppermute(value, AXES, moves)  7.82 us
    pallas_call x1, Pallas kernels, forward_products(): pl.pallas_call(forward_kernel, out_shape=(shape, shape, own), in_specs=[S...  3.35 us
    pallas_call x1, Pallas kernels, requests(): pl.pallas_call(functools.partial(request_kernel, cols, per_piece), out_sh...  2.8 us
  transfers between devices with their start and end apart: 10, of which 3 were waited for; matrix products, arithmetic and copies ran while one was open for 4% of the time, Pallas kernels for 11%

profile of v5, /device:TPU:7, one launch (start us, length us, event | category | flops | bytes accessed | tf_op | source)
XLA Modules:
  0.0 110.4 jit_solution(7103890289566868749)
XLA Ops:
  0.0 1.0 convert_bitcast_fusion.x_ref
  1.0 14.9 %collective-permute-start = (bf16[768,128]{1,0:T(8,128)(2,1)S(1)}, bf16[768,128]{1,0:T(8,128)(2,1)S(1)}, u32[]{:S(2)}, u32[]{:S(2)}) collective-permute-start(bf16[768,128]{1,0:T(8,128)(2,1)S(1)} %convert_bitcast_fusion.x_ref), channel_id=1, source_target_pairs={{0,12},{1,13},{2,14},{3,15},{4,16},{5,17},{6,18},{7,19},{8,20},{9,... | collective-permute-start | bytes 589832 | tf_op jit(solution)/shard_map/ppermute | solution.py:22
  17.1 2.8 %shard_map.64 = (s32[6,8,128]{2,1,0:T(8,128)}, s32[64]{0:T(128)}) custom-call(s32[3]{0:T(128)} %pad_add_fusion.place_ref, s32[64]{0:T(128)} %rows_ref.1, s32[1]{0:T(128)} %copy.11.live_ref), custom_call_target="tpu_custom_call" | custom-call | tf_op jit(solution)/shard_map/pallas_call | solution.py:96
  19.9 13.6 %all_to_all.25.asked_ref = s32[6,8,128]{2,1,0:T(8,128)S(1)} all-to-all(s32[6,8,128]{2,1,0:T(8,128)} %get-tuple-element.28), channel_id=1, replica_groups=mesh['row'=128,'col'=6] {'col'}, dimensions={0} | all-to-all | bytes 49152 | tf_op jit(solution)/shard_map/all_to_all | solution.py:318
  34.2 1.9 %shard_map.65 = (bf16[1536,128]{1,0:T(8,128)(2,1)}, bf16[1536,128]{1,0:T(8,128)(2,1)S(1)}, bf16[512,128]{1,0:T(8,128)(2,1)S(1)}) custom-call(s32[3]{0:T(128)S(1)} %copy-done.2, s32[6,8,128]{2,1,0:T(8,128)S(1)} %all_to_all.25.asked_ref, bf16[768,128]{1,0:T(8,128)(2,1)S(1)} %convert_bitcast_fusion.x_ref), custom_call_target="tpu_custom_call" | custom-call | tf_op jit(solution)/shard_map/pallas_call | solution.py:139
  36.1 5.4 %collective-permute-start.1 = (bf16[1536,128]{1,0:T(8,128)(2,1)S(1)}, bf16[1536,128]{1,0:T(8,128)(2,1)}, u32[]{:S(2)}, u32[]{:S(2)}) collective-permute-start(bf16[1536,128]{1,0:T(8,128)(2,1)S(1)} %pad_maximum_fusion.2), channel_id=1, source_target_pairs={{24,0},{25,1},{26,2},{27,3},{28,4},{29,5},{30,6},{31,7},{32,8},{33... | collective-permute-start | bytes 1179656 | tf_op jit(solution)/shard_map/ppermute | solution.py:22
  41.4 1.4 %collective-permute-start.2 = (bf16[768,128]{1,0:T(8,128)(2,1)S(1)}, bf16[768,128]{1,0:T(8,128)(2,1)}, u32[]{:S(2)}, u32[]{:S(2)}) collective-permute-start(bf16[768,128]{1,0:T(8,128)(2,1)S(1)} %collective-permute-done), channel_id=1, source_target_pairs={{60,12},{61,13},{62,14},{63,15},{64,16},{65,17},{66,18},{67,19},{6... | collective-permute-start | bytes 589832 | tf_op jit(solution)/shard_map/ppermute | solution.py:22
  44.3 4.3 %all-to-all-start.3 = ((bf16[6,256,128]{2,1,0:T(8,128)(2,1)}), bf16[6,256,128]{2,1,0:T(8,128)(2,1)}, u32[]{:S(2)}, u32[]{:S(2)}) async-start(bf16[6,256,128]{2,1,0:T(8,128)(2,1)} %bitcast.14), calls=%async_computation.3 | async-start | bytes 786432 | tf_op jit(solution)/shard_map/all_to_all | solution.py:56
  48.6 1.2 %pad_maximum_fusion.here_ref = bf16[3840,128]{1,0:T(8,128)(2,1)S(1)} fusion(bf16[768,128]{1,0:T(8,128)(2,1)} %collective-permute-done.2, bf16[1536,128]{1,0:T(8,128)(2,1)} %collective-permute-done.1, bf16[768,128]{1,0:T(8,128)(2,1)} %copy-done.7, bf16[768,128]{1,0:T(8,128)(2,1)S(1)} %convert_bitcast_fusion.x_ref), kind=kLoop, calls=%fused_computation | loop fusion | flops 3932160 | bytes 1966080 | tf_op jit(solution)/shard_map/concatenate | solution.py:325
  49.8 4.6 %collective-permute-start.3 = (bf16[3840,128]{1,0:T(8,128)(2,1)S(1)}, bf16[3840,128]{1,0:T(8,128)(2,1)}, u32[]{:S(2)}, u32[]{:S(2)}) collective-permute-start(bf16[3840,128]{1,0:T(8,128)(2,1)S(1)} %pad_maximum_fusion.here_ref), channel_id=1, source_target_pairs={{0,6},{1,7},{2,8},{3,9},{4,10},{5,11},{6,0},{7,1},{8,2},{9,3},{10,... | collective-permute-start | bytes 2949128 | tf_op jit(solution)/shard_map/ppermute | solution.py:22
  54.5 10.9 %all-to-all-done.3 = bf16[6,256,128]{2,1,0:T(8,128)(2,1)} async-done(((bf16[6,256,128]{2,1,0:T(8,128)(2,1)}), bf16[6,256,128]{2,1,0:T(8,128)(2,1)}, u32[]{:S(2)}, u32[]{:S(2)}) %all-to-all-start.3) | async-done | bytes 393248 | tf_op jit(solution)/shard_map/all_to_all | solution.py:56
  65.3 1.9 %shard_map.66 = bf16[528,128]{1,0:T(8,128)(2,1)S(1)} custom-call(s32[64]{0:T(128)S(1)} %copy-done.4, s32[64]{0:T(128)S(1)} %get-tuple-element.45.counts_ref, bf16[1536,128]{1,0:T(8,128)(2,1)} %bitcast.15.first_ref, bf16[1536,128]{1,0:T(8,128)(2,1)} %copy-done.6, bf16[512,128]{1,0:T(8,128)(2,1)S(1)} %get-tuple-element.34.own_ref, ...), custom_call_target="tpu_custom_call" | custom-call | tf_op jit(solution)/shard_map/pallas_call | solution.py:169
  67.3 8.8 %collective-permute-start.4 = (bf16[528,128]{1,0:T(8,128)(2,1)S(1)}, bf16[528,128]{1,0:T(8,128)(2,1)}, u32[]{:S(2)}, u32[]{:S(2)}) collective-permute-start(bf16[528,128]{1,0:T(8,128)(2,1)S(1)} %shard_map.66), channel_id=1, source_target_pairs={{0,12},{1,13},{2,14},{3,15},{4,16},{5,17},{6,18},{7,19},{8,20},{9,... | collective-permute-start | bytes 405512 | tf_op jit(solution)/shard_map/ppermute | solution.py:22
  76.1 3.3 %shard_map.67 = (bf16[1536,128]{1,0:T(8,128)(2,1)S(1)}, bf16[1536,128]{1,0:T(8,128)(2,1)}, bf16[512,128]{1,0:T(8,128)(2,1)S(1)}) custom-call(s32[64]{0:T(128)S(1)} %get-tuple-element.44.places_ref, s32[64]{0:T(128)S(1)} %copy-done.4, s32[64]{0:T(128)S(1)} %get-tuple-element.45.counts_ref, bf16[3840,128]{1,0:T(8,128)(2,1)S(1)} %pad_maximum_fusion.here_ref, ...), custom_call_target="tpu_custom_call" | custom-call | tf_op jit(solution)/shard_map/pallas_call | solution.py:208
  80.2 3.6 %all-to-all-start.4 = ((bf16[6,256,128]{2,1,0:T(8,128)(2,1)}), bf16[6,256,128]{2,1,0:T(8,128)(2,1)S(1)}, u32[]{:S(2)}, u32[]{:S(2)}) async-start(bf16[6,256,128]{2,1,0:T(8,128)(2,1)} %bitcast.32), calls=%async_computation.4 | async-start | bytes 786432 | tf_op jit(solution)/shard_map/all_to_all | solution.py:56
  83.8 0.9 pad_maximum_fusion.3
  84.7 2.3 %collective-permute-start.5 = (bf16[1056,128]{1,0:T(8,128)(2,1)S(1)}, bf16[1056,128]{1,0:T(8,128)(2,1)S(1)}, u32[]{:S(2)}, u32[]{:S(2)}) collective-permute-start(bf16[1056,128]{1,0:T(8,128)(2,1)S(1)} %pad_maximum_fusion.3), channel_id=1, source_target_pairs={{0,24},{1,25},{2,26},{3,27},{4,28},{5,29},{6,30},{7,31},{8,32},{9,... | collective-permute-start | bytes 811016 | tf_op jit(solution)/shard_map/ppermute | solution.py:22
  87.0 3.8 %collective-permute-start.6 = (bf16[528,128]{1,0:T(8,128)(2,1)}, bf16[528,128]{1,0:T(8,128)(2,1)S(1)}, u32[]{:S(2)}, u32[]{:S(2)}) collective-permute-start(bf16[528,128]{1,0:T(8,128)(2,1)} %collective-permute-done.4), channel_id=1, source_target_pairs={{0,48},{1,49},{2,50},{3,51},{4,52},{5,53},{6,54},{7,55},{8,56},{9,... | collective-permute-start | bytes 405512 | tf_op jit(solution)/shard_map/ppermute | solution.py:22
  90.8 7.8 %collective-permute-done.6 = bf16[528,128]{1,0:T(8,128)(2,1)S(1)} collective-permute-done((bf16[528,128]{1,0:T(8,128)(2,1)}, bf16[528,128]{1,0:T(8,128)(2,1)S(1)}, u32[]{:S(2)}, u32[]{:S(2)}) %collective-permute-start.6) | collective-permute-done | bytes 135200 | tf_op jit(solution)/shard_map/ppermute | solution.py:22
  98.6 1.0 pad_maximum_fusion.1.list_ref
  99.5 0.9 all-to-all-done.4
  100.5 6.1 %collective-permute-start.7 = (bf16[2640,128]{1,0:T(8,128)(2,1)S(1)}, bf16[2640,128]{1,0:T(8,128)(2,1)S(1)}, u32[]{:S(2)}, u32[]{:S(2)}) collective-permute-start(bf16[2640,128]{1,0:T(8,128)(2,1)S(1)} %pad_maximum_fusion.1.list_ref), channel_id=1, source_target_pairs={{0,6},{1,7},{2,8},{3,9},{4,10},{5,11},{6,0},{7,1},{8,2},{9,3},{10,... | collective-permute-start | bytes 2027528 | tf_op jit(solution)/shard_map/ppermute | solution.py:22
  106.6 2.1 %shard_map.68.start_ref = f32[8,96,128]{2,1,0:T(8,128)S(1)} custom-call(s32[3]{0:T(128)S(1)} %copy-done.3, s32[1]{0:T(128)} %bitcast.7.most_ref, s32[6,8,128]{2,1,0:T(8,128)S(1)} %all_to_all.25.asked_ref, bf16[1536,128]{1,0:T(8,128)(2,1)S(1)} %bitcast.31, bf16[1536,128]{1,0:T(8,128)(2,1)S(1)} %copy-done.5, bf16[512,128]{1,0:T(8,128)(2,1)S(1)} %get-tuple-element.38.own_ref, ...), custom_call_target="tpu_custom_call" | custom-call | tf_op jit(solution)/shard_map/pallas_call | solution.py:260
  108.7 1.7 %shard_map.69 = f32[768,128]{1,0:T(8,128)} custom-call(s32[3]{0:T(128)S(1)} %copy-done.3, f32[8,96,128]{2,1,0:T(8,128)S(1)} %shard_map.68.start_ref, bf16[2640,128]{1,0:T(8,128)(2,1)S(1)} %collective-permute-done.7.list_ref), custom_call_target="tpu_custom_call" | custom-call | tf_op jit(solution)/shard_map/pallas_call | solution.py:280
  (34 shorter events, 2.8 us)
Async XLA Ops:
  1.0 35.0 %collective-permute-start = (bf16[768,128]{1,0:T(8,128)(2,1)S(1)}, bf16[768,128]{1,0:T(8,128)(2,1)S(1)}, u32[]{:S(2)}, u32[]{:S(2)}) collective-permute-start(bf16[768,128]{1,0:T(8,128)(2,1)S(1)} %convert_bitcast_fusion.x_ref), channel_id=1, source_target_pairs={{0,12},{1,13},{2,14},{3,15},{4,16},{5,17},{6,18},{7,19},{8,20},{9,... | collective-permute-start | bytes 589832 | tf_op jit(solution)/shard_map/ppermute | solution.py:22
  33.6 0.6 copy-start.2
  36.0 12.5 %copy-start.7 = (bf16[768,128]{1,0:T(8,128)(2,1)}, bf16[768,128]{1,0:T(8,128)(2,1)S(1)}, u32[]{:S(2)}) copy-start(bf16[768,128]{1,0:T(8,128)(2,1)S(1)} %collective-permute-done) | copy-start | bytes 589828
  36.1 12.5 %collective-permute-start.1 = (bf16[1536,128]{1,0:T(8,128)(2,1)S(1)}, bf16[1536,128]{1,0:T(8,128)(2,1)}, u32[]{:S(2)}, u32[]{:S(2)}) collective-permute-start(bf16[1536,128]{1,0:T(8,128)(2,1)S(1)} %pad_maximum_fusion.2), channel_id=1, source_target_pairs={{24,0},{25,1},{26,2},{27,3},{28,4},{29,5},{30,6},{31,7},{32,8},{33... | collective-permute-start | bytes 1179656 | tf_op jit(solution)/shard_map/ppermute | solution.py:22
  41.4 7.1 %collective-permute-start.2 = (bf16[768,128]{1,0:T(8,128)(2,1)S(1)}, bf16[768,128]{1,0:T(8,128)(2,1)}, u32[]{:S(2)}, u32[]{:S(2)}) collective-permute-start(bf16[768,128]{1,0:T(8,128)(2,1)S(1)} %collective-permute-done), channel_id=1, source_target_pairs={{60,12},{61,13},{62,14},{63,15},{64,16},{65,17},{66,18},{67,19},{6... | collective-permute-start | bytes 589832 | tf_op jit(solution)/shard_map/ppermute | solution.py:22
  44.2 10.2 %copy-start.8 = (s32[64]{0:T(128)S(1)}, s32[64]{0:T(128)}, u32[]{:S(2)}) copy-start(s32[64]{0:T(128)} %param.13) | copy-start | bytes 772
  44.2 10.2 %copy-start.9 = (s32[64]{0:T(128)S(1)}, s32[64]{0:T(128)}, u32[]{:S(2)}) copy-start(s32[64]{0:T(128)} %param.14) | copy-start | bytes 772
  44.2 21.1 %copy-start = (bf16[64,128,128]{2,1,0:T(8,128)(2,1)S(1)}, bf16[64,128,128]{2,1,0:T(8,128)(2,1)}, u32[]{:S(2)}) copy-start(bf16[64,128,128]{2,1,0:T(8,128)(2,1)} %tiles_ref.3) | copy-start | bytes 6291460
  44.2 21.1 %copy-start.4 = (s32[64]{0:T(128)S(1)}, s32[64]{0:T(128)}, u32[]{:S(2)}) copy-start(s32[64]{0:T(128)} %get-tuple-element.29.places_ref.goals_ref) | copy-start | bytes 772
  44.3 4.3 %copy-start.6 = (bf16[1536,128]{1,0:T(8,128)(2,1)}, bf16[1536,128]{1,0:T(8,128)(2,1)S(1)}, u32[]{:S(2)}) copy-start(bf16[1536,128]{1,0:T(8,128)(2,1)S(1)} %get-tuple-element.46.second_ref) | copy-start | bytes 1179652
  44.3 21.1 %all-to-all-start.3 = ((bf16[6,256,128]{2,1,0:T(8,128)(2,1)}), bf16[6,256,128]{2,1,0:T(8,128)(2,1)}, u32[]{:S(2)}, u32[]{:S(2)}) async-start(bf16[6,256,128]{2,1,0:T(8,128)(2,1)} %bitcast.14), calls=%async_computation.3 | async-start | bytes 786432 | tf_op jit(solution)/shard_map/all_to_all | solution.py:56
  49.8 26.3 %collective-permute-start.3 = (bf16[3840,128]{1,0:T(8,128)(2,1)S(1)}, bf16[3840,128]{1,0:T(8,128)(2,1)}, u32[]{:S(2)}, u32[]{:S(2)}) collective-permute-start(bf16[3840,128]{1,0:T(8,128)(2,1)S(1)} %pad_maximum_fusion.here_ref), channel_id=1, source_target_pairs={{0,6},{1,7},{2,8},{3,9},{4,10},{5,11},{6,0},{7,1},{8,2},{9,3},{10,... | collective-permute-start | bytes 2949128 | tf_op jit(solution)/shard_map/ppermute | solution.py:22
  67.3 16.5 %collective-permute-start.4 = (bf16[528,128]{1,0:T(8,128)(2,1)S(1)}, bf16[528,128]{1,0:T(8,128)(2,1)}, u32[]{:S(2)}, u32[]{:S(2)}) collective-permute-start(bf16[528,128]{1,0:T(8,128)(2,1)S(1)} %shard_map.66), channel_id=1, source_target_pairs={{0,12},{1,13},{2,14},{3,15},{4,16},{5,17},{6,18},{7,19},{8,20},{9,... | collective-permute-start | bytes 405512 | tf_op jit(solution)/shard_map/ppermute | solution.py:22
  79.4 0.7 copy-start.1
  80.2 26.4 %copy-start.3 = (s32[3]{0:T(128)S(1)}, s32[3]{0:T(128)}, u32[]{:S(2)}) copy-start(s32[3]{0:T(128)} %pad_add_fusion.place_ref) | copy-start | bytes 40
  80.2 26.4 %copy-start.5 = (bf16[1536,128]{1,0:T(8,128)(2,1)S(1)}, bf16[1536,128]{1,0:T(8,128)(2,1)}, u32[]{:S(2)}) copy-start(bf16[1536,128]{1,0:T(8,128)(2,1)} %get-tuple-element.47.second_ref) | copy-start | bytes 1179652
  80.2 20.3 %all-to-all-start.4 = ((bf16[6,256,128]{2,1,0:T(8,128)(2,1)}), bf16[6,256,128]{2,1,0:T(8,128)(2,1)S(1)}, u32[]{:S(2)}, u32[]{:S(2)}) async-start(bf16[6,256,128]{2,1,0:T(8,128)(2,1)} %bitcast.32), calls=%async_computation.4 | async-start | bytes 786432 | tf_op jit(solution)/shard_map/all_to_all | solution.py:56
  84.7 13.9 %collective-permute-start.5 = (bf16[1056,128]{1,0:T(8,128)(2,1)S(1)}, bf16[1056,128]{1,0:T(8,128)(2,1)S(1)}, u32[]{:S(2)}, u32[]{:S(2)}) collective-permute-start(bf16[1056,128]{1,0:T(8,128)(2,1)S(1)} %pad_maximum_fusion.3), channel_id=1, source_target_pairs={{0,24},{1,25},{2,26},{3,27},{4,28},{5,29},{6,30},{7,31},{8,32},{9,... | collective-permute-start | bytes 811016 | tf_op jit(solution)/shard_map/ppermute | solution.py:22
  87.0 11.6 %collective-permute-start.6 = (bf16[528,128]{1,0:T(8,128)(2,1)}, bf16[528,128]{1,0:T(8,128)(2,1)S(1)}, u32[]{:S(2)}, u32[]{:S(2)}) collective-permute-start(bf16[528,128]{1,0:T(8,128)(2,1)} %collective-permute-done.4), channel_id=1, source_target_pairs={{0,48},{1,49},{2,50},{3,51},{4,52},{5,53},{6,54},{7,55},{8,56},{9,... | collective-permute-start | bytes 405512 | tf_op jit(solution)/shard_map/ppermute | solution.py:22
  100.5 8.2 %collective-permute-start.7 = (bf16[2640,128]{1,0:T(8,128)(2,1)S(1)}, bf16[2640,128]{1,0:T(8,128)(2,1)S(1)}, u32[]{:S(2)}, u32[]{:S(2)}) collective-permute-start(bf16[2640,128]{1,0:T(8,128)(2,1)S(1)} %pad_maximum_fusion.1.list_ref), channel_id=1, source_target_pairs={{0,6},{1,7},{2,8},{3,9},{4,10},{5,11},{6,0},{7,1},{8,2},{9,3},{10,... | collective-permute-start | bytes 2027528 | tf_op jit(solution)/shard_map/ppermute | solution.py:22
